TPU v7x, 32 devices: a whole 2x2x4 slice. The times are simulated.
32 devices in a mesh: shot: 2 (over x), sub: 16 (over z, y, core).
Axes of the slice: x: 2, y: 2, z: 4, core: 2. Of those that a mesh axis runs over, the one named last changes fastest.
Arguments:
- synthetic: float32 [16384, 256], P(('shot', 'sub')), parts along dimension 0, may hold values from -6 to 6
- observed: float32 [16384, 256], P(('shot', 'sub')), parts along dimension 0, may hold values from -6 to 6
- offsets: int32 [16384], P(('shot', 'sub')), parts along dimension 0, may hold values from 0 to 127
- lines: int32 [2, 16384], P(None, ('shot', 'sub')), parts along dimension 1, may hold values from 0 to 63, as said below
- owners: int32 [16384, 1], P(('shot', 'sub')), parts along dimension 0, may hold values from 0 to 15; in each aligned block of 512 rows (0 to 511, 512 to 1023, ...) at most 64 rows name the same one
- cells: int32 [16384], P(('shot', 'sub')), parts along dimension 0, may hold values from 0 to 65535
- taps: float32 [128], replicated, may hold values from -0.5 to 0.5
- line_taps: float32 [9], replicated, may hold values from -2 to 2
- velocity: float32 [128, 64, 128], P('sub'), may hold values from 1 to 2.5
- adjoint_old: float32 [256, 64, 128], P(('shot', 'sub')), parts along dimension 0, may hold values from -6 to 6
- adjoint_now: float32 [256, 64, 128], P(('shot', 'sub')), parts along dimension 0, may hold values from -6 to 6
- forward: float32 [4, 256, 64, 128], P(None, ('shot', 'sub')), parts along dimension 1, may hold values from -6 to 6
Outputs:
- adjoint_prior: float32 [256, 64, 128], P(('shot', 'sub')), parts along dimension 0
- adjoint_next: float32 [256, 64, 128], P(('shot', 'sub')), parts along dimension 0
- gradient: float32 [256, 64, 128], P(('shot', 'sub')), parts along dimension 0
There are 2 independent parts, one for each index of `shot`. A program takes and returns all parts, laid end to end along the dimension named above; an argument that names none is the same for every part. Nothing has to cross between parts.
Inputs may be any that keep to these rules, and one draw needn't show every extreme that they name: `owners`: among the receivers of one device at most 64 have the same owner, and in some devices some owner has exactly 64. `lines`: row 0 counts the receivers before a receiver on its line, row 1 those after it; each line is a run of at most 64 consecutive receivers, and some line has exactly 64.
All inputs are finite; a program needn't handle non-finite values.
Results may differ from a plain program's by a relative error of at most 0.00017.
Values sent between devices are 32-bit elements; how exact they have to be, the bound alone decides.
No kernel may reach another device: no remote copies, remote signals or barrier semaphores. Data moves between devices by JAX's collectives and lax.ppermute only.
A program may use at most 128 MiB of HBM per device.

v0:
```python
import jax
import jax.numpy as jnp
from jax import lax
from jax.sharding import PartitionSpec as P

NTAP = 128
SW = 4
STEPS = 2


COEF = (-205.0 / 72.0, 8.0 / 5.0, -1.0 / 5.0, 8.0 / 315.0, -1.0 / 560.0)
DT_OVER_H = 0.18


def extended(block, sides, width):
    for axis, dim in sides:
        count = lax.axis_size(axis)
        forward = [(i, i + 1) for i in range(count - 1)]
        backward = [(target, source) for source, target in forward]
        low = lax.ppermute(
            lax.slice_in_dim(block, block.shape[dim] - width, None, axis=dim), axis, forward
        )
        high = lax.ppermute(lax.slice_in_dim(block, 0, width, axis=dim), axis, backward)
        block = jnp.concatenate([low, block, high], axis=dim)
    return block


def moved(field, offset, axis):
    length = field.shape[axis]
    shape = list(field.shape)
    shape[axis] = abs(offset)
    zeros = jnp.zeros(tuple(shape), field.dtype)
    if offset > 0:
        return jnp.concatenate([lax.slice_in_dim(field, offset, length, axis=axis), zeros], axis)
    return jnp.concatenate([zeros, lax.slice_in_dim(field, 0, length + offset, axis=axis)], axis)


def wide_laplacian(padded):
    size_x = padded.shape[0] - 8
    centre = padded[4 : 4 + size_x]
    total = 3.0 * COEF[0] * centre
    for order in range(1, 5):
        total = total + COEF[order] * (
            padded[4 + order : 4 + order + size_x]
            + padded[4 - order : 4 - order + size_x]
            + moved(centre, order, 1)
            + moved(centre, -order, 1)
            + moved(centre, order, 2)
            + moved(centre, -order, 2)
        )
    return total


def crop(field, have, want):
    cut = have - want
    return field[cut : field.shape[0] - cut]


def cut_window(trace, start):
    return lax.dynamic_slice_in_dim(trace, start, NTAP + STEPS - 1)


def time_filter(window, taps):
    columns = [
        jnp.dot(window[:, lag : lag + NTAP], taps, precision=lax.Precision.HIGHEST)
        for lag in range(STEPS)
    ]
    return jnp.stack(columns, axis=1)


def line_filter(wide, lines, line_taps, count):
    before = lines[0]
    after = lines[1]
    total = jnp.zeros((count, wide.shape[1]), jnp.float32)
    for reach in range(-SW, SW + 1):
        neighbour = wide[SW + reach : SW + reach + count]
        if reach < 0:
            keep = before >= -reach
        elif reach > 0:
            keep = after >= reach
        else:
            keep = before >= 0
        total = total + jnp.where(keep[:, None], line_taps[reach + SW] * neighbour, 0.0)
    return total


def body(
    synthetic,
    observed,
    offsets,
    lines,
    owners,
    cells,
    taps,
    line_taps,
    velocity,
    adjoint_old,
    adjoint_now,
    forward,
):
    steps = forward.shape[0] - 2
    count = synthetic.shape[0]
    residual = synthetic - observed
    window = jax.vmap(cut_window)(residual, offsets)
    filtered = time_filter(window, taps)
    wide = extended(filtered, (("sub", 0),), SW)
    sources = line_filter(wide, lines, line_taps, count)
    devices = lax.axis_size("sub")
    owner_list = owners[:, 0]
    capacity = max(2, 2 * count // devices)
    one_hot = (owner_list[:, None] == jnp.arange(devices, dtype=jnp.int32)[None, :]).astype(
        jnp.int32
    )
    slot_rank = jnp.sum((jnp.cumsum(one_hot, axis=0) - 1) * one_hot, axis=1)
    target = owner_list * capacity + slot_rank
    send_values = jnp.zeros((devices * capacity, steps), jnp.float32).at[target].set(sources)
    send_cells = jnp.zeros((devices * capacity,), jnp.int32).at[target].set(cells)
    got_values, got_cells = (
        lax.all_to_all(
            send_values.reshape(devices, capacity, steps),
            "sub",
            split_axis=0,
            concat_axis=0,
            tiled=True,
        ),
        lax.all_to_all(
            send_cells.reshape(devices, capacity), "sub", split_axis=0, concat_axis=0, tiled=True
        ),
    )
    got_values = got_values.reshape(devices * capacity, steps)
    got_cells = got_cells.reshape(devices * capacity)
    block = velocity.size
    injected = jnp.zeros((steps, block), jnp.float32).at[:, got_cells].add(got_values.T)
    injected = injected.reshape((steps,) + velocity.shape)
    weight = 2.0 / (velocity * velocity * velocity)
    gradient = jnp.zeros_like(velocity)
    extent = 4 * (steps - 1)
    newer = extended(adjoint_now, (("sub", 0),), extent + 4)
    stacked = jnp.concatenate([adjoint_old[None], velocity[None], injected[: steps - 1]], axis=0)
    border = extended(stacked, (("sub", 1),), extent)
    older = border[0]
    older_extent = extent
    newer_extent = extent + 4
    for step in range(steps):
        margin = 4 * (steps - 1 - step)
        speed = crop(border[1], extent, margin)
        source = crop(border[2 + step], extent, margin) if step < steps - 1 else injected[step]
        fresh = (
            2.0 * crop(newer, newer_extent, margin)
            - crop(older, older_extent, margin)
            + (DT_OVER_H * speed) ** 2
            * (wide_laplacian(crop(newer, newer_extent, margin + 4)) + source)
        )
        inner = crop(fresh, margin, 0)
        gradient = gradient + weight * inner * (
            forward[step] - 2.0 * forward[step + 1] + forward[step + 2]
        )
        older, older_extent = (newer, newer_extent)
        newer, newer_extent = (fresh, margin)
    adjoint_prior = crop(older, older_extent, 0)
    return (adjoint_prior, newer, gradient)


def solution(mesh):
    return jax.shard_map(
        body,
        mesh=mesh,
        in_specs=(
            P(("shot", "sub"), None),
            P(("shot", "sub"), None),
            P(("shot", "sub")),
            P(None, ("shot", "sub")),
            P(("shot", "sub"), None),
            P(("shot", "sub")),
            P(),
            P(),
            P("sub", None, None),
            P(("shot", "sub"), None, None),
            P(("shot", "sub"), None, None),
            P(None, ("shot", "sub"), None, None),
        ),
        out_specs=(
            P(("shot", "sub"), None, None),
            P(("shot", "sub"), None, None),
            P(("shot", "sub"), None, None),
        ),
        check_vma=False,
    )
```

profile of v0, /device:TPU:0, one launch (start us, length us, event | category | flops | bytes accessed | tf_op | source)
XLA Modules:
  0.0 1145.2 jit_solution(17915846410082487032)
XLA Ops:
  0.7 2.5 collective-permute-start
  6.5 1028.8 %while.1 = (s32[]{:T(128)}, f32[512,256]{1,0:T(8,128)S(1)}, s32[512,2]{0,1:T(2,128)S(1)}, f32[512,129]{1,0:T(8,128)S(1)}, s32[]{:T(128)}, /*index=5*/s32[]{:T(128)}) while((s32[]{:T(128)}, f32[512,256]{1,0:T(8,128)S(1)}, s32[512,2]{0,1:T(2,128)S(1)}, f32[512,129]{1,0:T(8,128)S(1)}, s32[]{:T(128)}, /*index=5*/s32[]{:T(128)}) %tuple.61), condition=%wide.while_cond, body=%wide.while_body.sunk | while | flops 2 | bytes 2177 | solution.py:60
  7.1 1.4 dynamic-slice.7
  9.1 1.4 dynamic-slice.7
  11.1 1.4 dynamic-slice.7
  13.1 1.4 dynamic-slice.7
  15.1 1.4 dynamic-slice.7
  17.1 1.4 dynamic-slice.7
  19.2 1.4 dynamic-slice.7
  21.2 1.4 dynamic-slice.7
  23.2 1.4 dynamic-slice.7
  25.2 1.4 dynamic-slice.7
  27.2 1.4 dynamic-slice.7
  29.2 1.4 dynamic-slice.7
  31.2 1.4 dynamic-slice.7
  33.2 1.4 dynamic-slice.7
  35.2 1.4 dynamic-slice.7
  37.2 1.4 dynamic-slice.7
  39.2 1.4 dynamic-slice.7
  41.3 1.4 dynamic-slice.7
  43.3 1.4 dynamic-slice.7
  1036.2 5.2 collective-permute-start.2
  1044.2 2.6 scatter_custom_fusion
  1047.5 9.2 all-to-all-start
  1057.6 5.7 fusion.77
  1063.5 1.8 scatter_custom_fusion.1
  1066.2 6.0 all-to-all-start.1
  1073.5 5.1 all-to-all-done.1
  1080.1 19.9 %scatter_custom_fusion.2 = f32[2,65536]{0,1:T(8,128)} fusion(s32[1024]{0:T(1024)S(1)} %bitcast.115, f32[1024,2]{1,0:T(8,128)S(1)} %bitcast.108, f32[]{:T(128)} %constant.19.clone.1), kind=kCustom, calls=%fused_computation.6 | custom fusion | flops 2048 | bytes 524292 | tf_op jit(solution)/shard_map/scatter-add | solution.py:133
  1100.0 34.9 %slice_reduce_fusion = (f32[65536]{0:T(1024)S(1)}, f32[65536]{0:T(1024)S(1)}) fusion(f32[2,65536]{0,1:T(8,128)} %scatter_custom_fusion.2), kind=kLoop, calls=%fused_computation.4 | loop fusion | bytes 1048576 | tf_op jit(solution)/shard_map/slice | solution.py:147
  1135.0 1.8 collective-permute-start.4
  1143.7 1.5 fusion.61
  (2108 shorter events, 1013.0 us)
Async XLA Ops:
  0.6 1034.7 %copy-start = (f32[128]{0:T(128)S(1)}, f32[128]{0:T(128)}, u32[]{:S(2)}) copy-start(f32[128]{0:T(128)} %param.18) | copy-start | bytes 1540
  0.6 1042.0 %copy-start.6 = (s32[512,1]{0,1:T(1,128)S(1)}, s32[512,1]{0,1:T(1,128)}, u32[]{:S(2)}) copy-start(s32[512,1]{0,1:T(1,128)} %param.16) | copy-start | bytes 6148
  0.7 1056.1 %copy-start.5 = (f32[9]{0:T(128)S(1)}, f32[9]{0:T(128)}, u32[]{:S(2)}) copy-start(f32[9]{0:T(128)} %param.19) | copy-start | bytes 112
  0.7 1056.8 %copy-start.7 = (s32[2,512]{1,0:T(2,128)S(1)}, s32[2,512]{1,0:T(2,128)}, u32[]{:S(2)}) copy-start(s32[2,512]{1,0:T(2,128)} %param.15) | copy-start | bytes 12292
  0.7 1137.5 %collective-permute-start = (f32[8,64,128]{2,1,0:T(8,128)}, f32[8,64,128]{2,1,0:T(8,128)S(1)}, u32[]{:S(2)}, u32[]{:S(2)}) collective-permute-start(f32[8,64,128]{2,1,0:T(8,128)} %param.22), channel_id=1, source_target_pairs={{0,1},{1,2},{2,3},{3,4},{4,5},{5,6},{6,7},{7,8},{8,9},{9,10},{10,1... | collective-permute-start | bytes 786440 | tf_op jit(solution)/shard_map/ppermute | solution.py:20
  3.2 1135.1 %collective-permute-start.1 = (f32[8,64,128]{2,1,0:T(8,128)}, f32[8,64,128]{2,1,0:T(8,128)S(1)}, u32[]{:S(2)}, u32[]{:S(2)}) collective-permute-start(f32[8,64,128]{2,1,0:T(8,128)} %param.22), channel_id=1, source_target_pairs={{1,0},{2,1},{3,2},{4,3},{5,4},{6,5},{7,6},{8,7},{9,8},{10,9},{11,1... | collective-permute-start | bytes 786440 | tf_op jit(solution)/shard_map/ppermute | solution.py:23
  1036.2 21.3 %collective-permute-start.2 = (f32[4,2]{0,1:T(2,128)S(1)}, f32[4,2]{0,1:T(2,128)S(1)}, u32[]{:S(2)}, u32[]{:S(2)}) collective-permute-start(f32[4,2]{0,1:T(2,128)S(1)} %get-tuple-element.71), channel_id=1, source_target_pairs={{0,1},{1,2},{2,3},{3,4},{4,5},{5,6},{6,7},{7,8},{8,9},{9,10},{10,1... | collective-permute-start | bytes 104 | tf_op jit(solution)/shard_map/ppermute | solution.py:20
  1041.4 16.2 %collective-permute-start.3 = (f32[4,2]{0,1:T(2,128)S(1)}, f32[4,2]{0,1:T(2,128)S(1)}, u32[]{:S(2)}, u32[]{:S(2)}) collective-permute-start(f32[4,2]{0,1:T(2,128)S(1)} %get-tuple-element.72), channel_id=1, source_target_pairs={{1,0},{2,1},{3,2},{4,3},{5,4},{6,5},{7,6},{8,7},{9,8},{10,9},{11,1... | collective-permute-start | bytes 104 | tf_op jit(solution)/shard_map/ppermute | solution.py:23
  1047.5 18.7 %all-to-all-start = ((s32[16,1,64]{2,1,0:T(1,128)}), s32[16,1,64]{2,1,0:T(1,128)S(1)}, u32[]{:S(2)}, u32[]{:S(2)}) async-start(s32[16,1,64]{2,1,0:T(1,128)} %all_to_all.9), calls=%async_computation | async-start | bytes 16384 | tf_op jit(solution)/shard_map/all_to_all | solution.py:126
  1066.2 12.3 %all-to-all-start.1 = ((f32[16,1,128]{2,1,0:T(1,128)}), f32[16,1,128]{2,1,0:T(1,128)S(1)}, u32[]{:S(2)}, u32[]{:S(2)}) async-start(f32[16,1,128]{2,1,0:T(1,128)} %reshape.217), calls=%async_computation.1 | async-start | bytes 16384 | tf_op jit(solution)/shard_map/all_to_all | solution.py:119
  1100.0 34.9 %copy-start.2 = (f32[8,64,128]{2,1,0:T(8,128)S(1)}, f32[8,64,128]{2,1,0:T(8,128)}, u32[]{:S(2)}) copy-start(f32[8,64,128]{2,1,0:T(8,128)} %param.20) | copy-start | bytes 786436
  1100.0 34.9 %copy-start.4 = (f32[8,64,128]{2,1,0:T(8,128)S(1)}, f32[8,64,128]{2,1,0:T(8,128)}, u32[]{:S(2)}) copy-start(f32[8,64,128]{2,1,0:T(8,128)} %param.21) | copy-start | bytes 786436
  1134.9 3.3 copy-start.1
  1135.0 4.5 collective-permute-start.4
  1136.9 3.7 collective-permute-start.5
  1142.5 1.2 copy-start.3
where the time goes:
time: 1160 us; the launch traced here: 1150 us
  local copies, waits for them, and re-layouts  1070 us (92%)
  other arithmetic  33.5 us (3%)
  starting transfers between devices  28.6 us (2%)
    gather x2048, local copies, waits for them, and re-layouts  1020 us
    slice x1, local copies, waits for them, and re-layouts, body(): injected[step]  34.9 us
  transfers between devices with their start and end apart: 8, of which 2 were waited for; matrix products, arithmetic and copies ran while one was open for 96% of the time, Pallas kernels for 0%

commit v1 on v0

v1 whole, which is shorter than its diff:
```python
import functools

import jax
import jax.numpy as jnp
from jax import lax
from jax.experimental import pallas as pl
from jax.experimental.pallas import tpu as pltpu
from jax.sharding import PartitionSpec as P

SW = 4
STEPS = 2
REACH = 4
LANES = 128
EDGE = 2 * SW

COEF = (-205.0 / 72.0, 8.0 / 5.0, -1.0 / 5.0, 8.0 / 315.0, -1.0 / 560.0)
DT_OVER_H = 0.18

VMEM = pl.BlockSpec(memory_space=pltpu.VMEM)
SMEM = pl.BlockSpec(memory_space=pltpu.SMEM)
NT_DIMS = (((1,), (1,)), ((), ()))


def parts_of(value, count):
    parts = []
    for _ in range(count):
        part = value.astype(jnp.bfloat16).astype(jnp.float32)
        parts.append(part)
        value = value - part
    return parts


def iota(shape, axis):
    return lax.broadcasted_iota(jnp.int32, shape, axis)


def pack_kernel(
    devices, cap, block, syn, obs, off, lines, own, cells, taps, line_taps, send
):
    me = lax.axis_index("sub")
    count, samples = syn.shape
    ntap = taps.shape[1]
    residual = syn[...] - obs[...]
    starts = -(-(samples - ntap + 1) // 8) * 8
    row = jnp.concatenate([taps[...], jnp.zeros((1, samples - ntap), jnp.float32)], axis=1)
    toeplitz = pltpu.roll(
        jnp.broadcast_to(row, (starts, samples)), 0, 1, stride=1, stride_axis=0
    )
    all_starts = lax.dot_general(
        toeplitz,
        residual,
        NT_DIMS,
        precision=lax.Precision.HIGHEST,
        preferred_element_type=jnp.float32,
    )
    start = iota((starts, count), 0)
    offset = off[...]
    filtered = [
        jnp.sum(jnp.where(start == offset + step, all_starts, 0.0), axis=0, keepdims=True)
        for step in range(STEPS)
    ]
    both = jnp.concatenate(filtered + [jnp.zeros((8 - STEPS, count), jnp.float32)], axis=0)
    place = iota((1, count), 1)
    before = lines[0:1, :]
    after = lines[1:2, :]
    sources = jnp.zeros((8, count), jnp.float32)
    for reach in range(-SW, SW + 1):
        term = line_taps[reach + SW] * (
            pltpu.roll(both, (-reach) % count, 1) if reach else both
        )
        if reach < 0:
            keep = (before >= -reach) & (place >= -reach)
        elif reach > 0:
            keep = (after >= reach) & (place < count - reach)
        else:
            keep = before >= 0
        sources = sources + jnp.where(keep, term, 0.0)
    owner = own[...]
    hot = iota((devices, count), 0) == owner
    hot_f = hot.astype(jnp.float32)
    earlier = (iota((count, count), 0) < iota((count, count), 1)).astype(jnp.float32)
    ranks = jnp.dot(
        hot_f.astype(jnp.bfloat16),
        earlier.astype(jnp.bfloat16),
        preferred_element_type=jnp.float32,
    )
    rank = jnp.sum(jnp.where(hot, ranks, 0.0), axis=0, keepdims=True).astype(jnp.int32)
    cell = cells[...]
    high = (cell >> 8).astype(jnp.float32)
    low = (cell & 255).astype(jnp.float32)
    pieces = parts_of(sources[0:1], 3) + parts_of(sources[1:2], 3) + [high, low]
    spread = jnp.concatenate([hot_f * piece for piece in pieces], axis=0).astype(jnp.bfloat16)
    pack = LANES // cap
    lane = iota((LANES, count), 0)
    slot = (lane == rank + (me % pack) * cap).astype(jnp.float32).astype(jnp.bfloat16)
    out = lax.dot_general(spread, slot, NT_DIMS, preferred_element_type=jnp.float32)
    part = [out[k * devices : (k + 1) * devices] for k in range(8)]
    value0 = part[0] + part[1] + part[2]
    value1 = part[3] + part[4] + part[5]
    where = 256.0 * part[6] + part[7]
    none = jnp.zeros((1, LANES), jnp.float32)

    def to_upper(rows):
        return pltpu.roll(jnp.concatenate([none, rows[:-1]], axis=0), LANES // 2, 1)

    def to_lower(rows):
        return pltpu.roll(jnp.concatenate([rows[1:], none], axis=0), LANES // 2, 1)

    send[:, 0, :] = value0 + to_upper(value0)
    send[:, 1, :] = where + to_upper(where)
    send[:, 2, :] = value1 + to_lower(value0)
    send[:, 3, :] = to_lower(where)
    group = LANES // EDGE
    count_ = jnp.where(place < SW, before, after).astype(jnp.float32)
    edge_rows = (
        parts_of(both[0:1], 3)
        + parts_of(both[1:2], 3)
        + [owner.astype(jnp.float32), high, low, count_]
    )
    edge_rows = jnp.concatenate(
        edge_rows + [jnp.zeros((16 - len(edge_rows), count), jnp.float32)], axis=0
    ).astype(jnp.bfloat16)
    edge_lane = jnp.where(
        place < SW, place, jnp.where(place >= count - SW, place - count + EDGE, -LANES)
    )
    chosen = (lane == edge_lane + (me % group) * EDGE).astype(jnp.float32).astype(jnp.bfloat16)
    edge = lax.dot_general(edge_rows, chosen, NT_DIMS, preferred_element_type=jnp.float32)
    edge_cell = edge[6:7] * float(block) + 256.0 * edge[7:8] + edge[8:9]
    shape = (devices, LANES)
    send[:, 4, :] = jnp.broadcast_to(edge[0:1] + edge[1:2] + edge[2:3], shape)
    send[:, 5, :] = jnp.broadcast_to(edge[3:4] + edge[4:5] + edge[5:6], shape)
    send[:, 6, :] = jnp.broadcast_to(edge_cell, shape)
    send[:, 7, :] = jnp.broadcast_to(edge[9:10], shape)


PAD = 8


def laplacian_plane(field, x, size_y):
    centre = field[x, PAD : PAD + size_y, :]
    lanes = centre.shape[1]
    lane = iota(centre.shape, 1)
    total = 3.0 * COEF[0] * centre
    for k in range(1, 5):
        near = field[x + k, PAD : PAD + size_y, :] + field[x - k, PAD : PAD + size_y, :]
        near = near + field[x, PAD + k : PAD + k + size_y, :]
        near = near + field[x, PAD - k : PAD - k + size_y, :]
        near = near + jnp.where(lane < lanes - k, pltpu.roll(centre, lanes - k, 1), 0.0)
        near = near + jnp.where(lane >= k, pltpu.roll(centre, k, 1), 0.0)
        total = total + COEF[k] * near
    return total


def first_kernel(
    from_pair, from_next, old, now, vel, fwd, free, scale, weight0, weight1, wide, edges
):
    odd = lax.axis_index("sub") % 2
    size_x, size_y, lanes = old.shape
    zeros = jnp.zeros((wide.shape[0], PAD, lanes), jnp.float32)
    wide[:, 0:PAD, :] = zeros
    wide[:, PAD + size_y :, :] = zeros
    inside = slice(PAD, PAD + size_y)
    wide[2 * REACH : 2 * REACH + size_x, inside, :] = now[...]
    above = 2 * REACH + size_x

    def place(lower, upper):
        wide[0 : 2 * REACH, inside, :] = lower[0 : 2 * REACH]
        wide[above : above + 2 * REACH, inside, :] = upper[0 : 2 * REACH]
        edges[0] = lower[2 * REACH : 3 * REACH]
        edges[1] = lower[3 * REACH : 4 * REACH]
        edges[2] = upper[2 * REACH : 3 * REACH]
        edges[3] = upper[3 * REACH : 4 * REACH]

    @pl.when(odd == 0)
    def _():
        place(from_next, from_pair)

    @pl.when(odd == 1)
    def _():
        place(from_pair, from_next)

    def step(out_x, older, speed):
        factor = DT_OVER_H * speed
        factor = factor * factor
        scale[out_x] = factor
        x = out_x + REACH
        free[out_x] = (
            2.0 * wide[x, inside, :] - older + factor * laplacian_plane(wide, x, size_y)
        )

    @pl.loop(0, REACH)
    def _(x):
        step(x, edges[0, x], edges[1, x])
        step(x + REACH + size_x, edges[2, x], edges[3, x])

    @pl.loop(0, size_x)
    def _(x):
        speed = vel[x]
        step(x + REACH, old[x], speed)
        weight = 2.0 / (speed * speed * speed)
        f1 = fwd[1, x]
        f2 = fwd[2, x]
        weight0[x] = weight * (fwd[0, x] - 2.0 * f1 + f2)
        weight1[x] = weight * (f1 - 2.0 * f2 + fwd[3, x])


def second_kernel(
    devices,
    cap,
    got,
    line_taps,
    free,
    scale,
    now,
    weight0,
    weight1,
    prior,
    last,
    gradient,
    field,
    source1,
):
    me = lax.axis_index("sub")
    size_x, size_y, lanes = now.shape
    rows = size_x * size_y
    halo = REACH * size_y
    block = rows * lanes
    pack = LANES // cap
    lane8 = iota((8, LANES), 1)

    group = LANES // EDGE
    edge_parts = []
    for g in range(-(-devices // group)):
        total = got[g * group]
        for i in range(g * group + 1, min(devices, (g + 1) * group)):
            total = total + got[i]
        edge_parts.append(total)
    edge = jnp.concatenate(edge_parts, axis=1)
    width = edge.shape[1]
    spot = iota((8, width), 1)
    e = spot % EDGE
    count = edge[7:8]
    missing = jnp.zeros((8, width), jnp.float32)
    for reach in range(-SW, SW + 1):
        if reach == 0:
            continue
        if reach < 0:
            crosses = (e < -reach) & (spot >= -reach)
        else:
            crosses = (e >= EDGE - reach) & (spot < width - reach)
        keep = crosses & (count >= float(abs(reach)))
        missing = missing + jnp.where(
            keep, line_taps[reach + SW] * pltpu.roll(edge, (-reach) % width, 1), 0.0
        )
    edge_cell = edge[6:7].astype(jnp.int32) - me * block

    zs = iota((LANES, LANES), 0)
    row_own = iota((rows, LANES), 0)
    row_halo = iota((halo, LANES), 0)

    def hot_rows(cell, shift, index):
        at = (cell >> (lanes.bit_length() - 1)) + shift
        return (index == at).astype(jnp.float32).astype(jnp.bfloat16)

    def spread(cell, values):
        hot = zs == (cell & (lanes - 1))
        stack = []
        for value in values:
            for part in parts_of(value, 2):
                stack.append(jnp.where(hot, part, 0.0))
        return jnp.concatenate(stack, axis=0).astype(jnp.bfloat16)

    own_a, own_b, low_a, low_b, high_a, high_b = [], [], [], [], [], []

    for g in range(devices // pack):
        tiles = [got[g * pack + q] for q in range(pack)]
        mine, other = tiles[0], tiles[pack // 2]
        for q in range(1, pack):
            later = lane8 >= q * cap
            mine = jnp.where(later, tiles[q], mine)
            other = jnp.where(later, tiles[(q + pack // 2) % pack], other)
        cell = mine[1:2].astype(jnp.int32)
        own_a.append(hot_rows(cell, 0, row_own))
        own_b.append(spread(cell, [mine[0:1], mine[2:3]]))
        cell = other[1:2].astype(jnp.int32)
        low_a.append(hot_rows(cell, halo - rows, row_halo))
        low_b.append(spread(cell, [other[0:1]]))
        cell = other[3:4].astype(jnp.int32)
        high_a.append(hot_rows(cell, 0, row_halo))
        high_b.append(spread(cell, [other[2:3]]))
    for g in range(width // LANES):
        at = slice(g * LANES, (g + 1) * LANES)
        cell = edge_cell[:, at]
        b = spread(cell, [missing[4:5, at], missing[5:6, at]])
        own_a.append(hot_rows(cell, 0, row_own))
        own_b.append(b)
        low_a.append(hot_rows(cell, halo, row_halo))
        low_b.append(b[: 2 * LANES])
        high_a.append(hot_rows(cell, -rows, row_halo))
        high_b.append(b[: 2 * LANES])

    def inject(a, b):
        return lax.dot_general(
            jnp.concatenate(a, axis=1),
            jnp.concatenate(b, axis=1),
            NT_DIMS,
            preferred_element_type=jnp.float32,
        )

    zeros = jnp.zeros((field.shape[0], PAD, lanes), jnp.float32)
    field[:, 0:PAD, :] = zeros
    field[:, PAD + size_y :, :] = zeros
    inside = slice(PAD, PAD + size_y)
    top = REACH + size_x

    out = inject(own_a, own_b)
    first = (out[:, 0:lanes] + out[:, lanes : 2 * lanes]).reshape(size_x, size_y, lanes)
    source1[...] = (out[:, 2 * lanes : 3 * lanes] + out[:, 3 * lanes :]).reshape(
        size_x, size_y, lanes
    )
    fresh = free[REACH:top] + scale[REACH:top] * first
    prior[...] = fresh
    field[REACH:top, inside, :] = fresh
    out = inject(low_a, low_b)
    first = (out[:, 0:lanes] + out[:, lanes:]).reshape(REACH, size_y, lanes)
    field[0:REACH, inside, :] = free[0:REACH] + scale[0:REACH] * first
    out = inject(high_a, high_b)
    first = (out[:, 0:lanes] + out[:, lanes:]).reshape(REACH, size_y, lanes)
    field[top:, inside, :] = free[top:] + scale[top:] * first

    @pl.loop(0, size_x)
    def _(x):
        at = x + REACH
        fresh = field[at, inside, :]
        following = (
            2.0 * fresh
            - now[x]
            + scale[at] * (laplacian_plane(field, at, size_y) + source1[x])
        )
        last[x] = following
        gradient[x] = weight0[x] * fresh + weight1[x] * following


def body(
    synthetic,
    observed,
    offsets,
    lines,
    owners,
    cells,
    taps,
    line_taps,
    velocity,
    adjoint_old,
    adjoint_now,
    forward,
):
    count = synthetic.shape[0]
    size_x, size_y, lanes = velocity.shape
    devices = lax.axis_size("sub")
    me = lax.axis_index("sub")
    cap = max(2, 2 * count // devices)
    f32 = jnp.float32

    pair = [(i, i ^ 1) for i in range(devices)]
    following = [(i, i + 1) for i in range(1, devices - 1, 2)]
    following = following + [(b, a) for a, b in following]

    def edge_planes(start):
        return jnp.concatenate(
            [
                adjoint_now,
                lax.dynamic_slice_in_dim(adjoint_old, start, REACH, 0),
                lax.dynamic_slice_in_dim(velocity, start, REACH, 0),
            ],
            axis=0,
        )

    odd = me % 2
    top = size_x - REACH
    from_pair = lax.ppermute(edge_planes(jnp.where(odd == 0, top, 0)), "sub", pair)
    from_next = lax.ppermute(edge_planes(jnp.where(odd == 0, 0, top)), "sub", following)

    send = pl.pallas_call(
        functools.partial(pack_kernel, devices, cap, velocity.size),
        out_shape=jax.ShapeDtypeStruct((devices, 8, LANES), f32),
        in_specs=[VMEM] * 7 + [SMEM],
        out_specs=VMEM,
        name="pack",
    )(
        synthetic,
        observed,
        offsets.reshape(1, count),
        lines,
        owners.reshape(1, count),
        cells.reshape(1, count),
        taps.reshape(1, -1),
        line_taps,
    )
    got = lax.all_to_all(send, "sub", split_axis=0, concat_axis=0, tiled=True)

    plane = (size_y, lanes)
    outer = size_x + 2 * REACH
    free, scale, weight0, weight1 = pl.pallas_call(
        first_kernel,
        out_shape=(
            jax.ShapeDtypeStruct((outer,) + plane, f32),
            jax.ShapeDtypeStruct((outer,) + plane, f32),
            jax.ShapeDtypeStruct((size_x,) + plane, f32),
            jax.ShapeDtypeStruct((size_x,) + plane, f32),
        ),
        in_specs=[VMEM] * 6,
        out_specs=(VMEM,) * 4,
        scratch_shapes=[
            pltpu.VMEM((size_x + 4 * REACH, size_y + 2 * PAD, lanes), f32),
            pltpu.VMEM((4, REACH) + plane, f32),
        ],
        name="first",
    )(from_pair, from_next, adjoint_old, adjoint_now, velocity, forward)

    field = jax.ShapeDtypeStruct((size_x,) + plane, f32)
    return pl.pallas_call(
        functools.partial(second_kernel, devices, cap),
        out_shape=(field, field, field),
        in_specs=[VMEM, SMEM] + [VMEM] * 5,
        out_specs=(VMEM,) * 3,
        scratch_shapes=[
            pltpu.VMEM((outer, size_y + 2 * PAD, lanes), f32),
            pltpu.VMEM((size_x,) + plane, f32),
        ],
        name="second",
    )(got, line_taps, free, scale, adjoint_now, weight0, weight1)


def solution(mesh):
    return jax.shard_map(
        body,
        mesh=mesh,
        in_specs=(
            P(("shot", "sub"), None),
            P(("shot", "sub"), None),
            P(("shot", "sub")),
            P(None, ("shot", "sub")),
            P(("shot", "sub"), None),
            P(("shot", "sub")),
            P(),
            P(),
            P("sub", None, None),
            P(("shot", "sub"), None, None),
            P(("shot", "sub"), None, None),
            P(None, ("shot", "sub"), None, None),
        ),
        out_specs=(
            P(("shot", "sub"), None, None),
            P(("shot", "sub"), None, None),
            P(("shot", "sub"), None, None),
        ),
        check_vma=False,
    )
```

time: 1160 us -> 31 us (0.03)
  the two profiles are of different devices: /device:TPU:0 before, /device:TPU:9 now
where the time goes in v1:
time: 31 us; the launch traced here: 30.7 us
  Pallas kernels  12.8 us (41%)
  starting transfers between devices  9.19 us (30%)
  waiting for transfers between devices  5.25 us (17%)
  local copies, waits for them, and re-layouts  2.62 us (8%)
  between operations  0.7 us (2%)
    all_to_all x1, starting transfers between devices, body(): got = lax.all_to_all(send, 'sub', split_axis=0, concat_axis=0, tiled=True)  5.41 us
    ppermute x1, waiting for transfers between devices, body(): lax.ppermute(edge_planes(jnp.where(odd == 0, 0, top)), 'sub', following)  5.24 us
    pallas_call x1, Pallas kernels, body(): pl.pallas_call(first_kernel, out_shape=(jax.ShapeDtypeStruct((outer,) + p...  5.05 us
    pallas_call x1, Pallas kernels, body(): pl.pallas_call(functools.partial(second_kernel, devices, cap), out_shape=...  4.77 us
    ppermute x1, starting transfers between devices, body(): lax.ppermute(edge_planes(jnp.where(odd == 0, 0, top)), 'sub', following)  3.05 us
    pallas_call x1, Pallas kernels, body(): pl.pallas_call(functools.partial(pack_kernel, devices, cap, velocity.size...  3 us
    unnamed x8, local copies, waits for them, and re-layouts  1.44 us
    dynamic_slice x1, local copies, waits for them, and re-layouts, edge_planes(): lax.dynamic_slice_in_dim(velocity, start, REACH, 0)  1.18 us
  transfers between devices with their start and end apart: 3, of which 1 were waited for; matrix products, arithmetic and copies ran while one was open for 0% of the time, Pallas kernels for 26%

profile of v1, /device:TPU:9, one launch (start us, length us, event | category | flops | bytes accessed | tf_op | source)
XLA Modules:
  0.0 30.7 jit_solution(8939201663868615764)
XLA Ops:
  0.6 0.0 copy-start
  0.7 1.2 %constant_dynamic-slice_fusion = (f32[4,64,128]{2,1,0:T(8,128)S(1)}, f32[4,64,128]{2,1,0:T(8,128)S(1)}, f32[4,64,128]{2,1,0:T(8,128)S(1)}, f32[4,64,128]{2,1,0:T(8,128)S(1)}) fusion(f32[8,64,128]{2,1,0:T(8,128)} %vel.1, s32[]{:T(128)S(6)} %select_n.20, s32[]{:T(128)S(6)} %select_n.19, f32[8,64,128]{2,1,0:T(8,128)} %old.1), kind=kLoop, calls=%fused_computation.4 | loop fusion | bytes 1048584 | tf_op jit(solution)/shard_map/dynamic_slice | solution.py:374
  1.8 0.0 copy-done
  1.8 0.1 fusion.1
  2.0 0.7 %collective-permute-start = (f32[16,64,128]{2,1,0:T(8,128)S(1)}, f32[16,64,128]{2,1,0:T(8,128)S(1)}, u32[]{:S(2)}, u32[]{:S(2)}) collective-permute-start(f32[16,64,128]{2,1,0:T(8,128)S(1)} %get-tuple-element.12), channel_id=1, source_target_pairs={{0,1},{1,0},{2,3},{3,2},{4,5},{5,4},{6,7},{7,6},{8,9},{9,8},{10,11... | collective-permute-start | bytes 1572872 | tf_op jit(solution)/shard_map/ppermute | solution.py:381
  2.7 3.0 %collective-permute-start.1 = (f32[16,64,128]{2,1,0:T(8,128)S(1)}, f32[16,64,128]{2,1,0:T(8,128)S(1)}, u32[]{:S(2)}, u32[]{:S(2)}) collective-permute-start(f32[16,64,128]{2,1,0:T(8,128)S(1)} %get-tuple-element.11), channel_id=1, source_target_pairs={{1,2},{3,4},{5,6},{7,8},{9,10},{11,12},{13,14},{2,1},{4,3},{6,5},{... | collective-permute-start | bytes 1572872 | tf_op jit(solution)/shard_map/ppermute | solution.py:382
  5.8 3.0 %pack.1 = f32[16,8,128]{2,1,0:T(8,128)} custom-call(f32[512,256]{1,0:T(8,128)} %syn.1, f32[512,256]{1,0:T(8,128)} %obs.1, s32[1,512]{1,0:T(1,128)} %bitcast.4, s32[2,512]{1,0:T(2,128)} %lines.1, s32[1,512]{1,0:T(1,128)} %bitcast.5, s32[1,512]{1,0:T(1,128)} %bitcast.6, f32[1,128]{1,0:T(1,128)} %bitcast.7, f32[9]{0:T(128)} %line_taps.3), custom_call_target="tpu_custom_call" | custom-call | tf_op jit(solution)/shard_map/pack/pallas_call | solution.py:384
  8.8 5.4 %all-to-all-start = ((f32[16,8,128]{2,1,0:T(8,128)}), f32[16,8,128]{2,1,0:T(8,128)S(1)}, u32[]{:S(2)}, u32[]{:S(2)}) async-start(f32[16,8,128]{2,1,0:T(8,128)} %pack.1), calls=%async_computation | async-start | bytes 131072 | tf_op jit(solution)/shard_map/all_to_all | solution.py:400
  14.2 0.0 collective-permute-done.from_pair
  14.2 0.0 copy-start.1
  14.2 5.2 %collective-permute-done.1.from_next = f32[16,64,128]{2,1,0:T(8,128)S(1)} collective-permute-done((f32[16,64,128]{2,1,0:T(8,128)S(1)}, f32[16,64,128]{2,1,0:T(8,128)S(1)}, u32[]{:S(2)}, u32[]{:S(2)}) %collective-permute-start.1) | collective-permute-done | bytes 524320 | tf_op jit(solution)/shard_map/ppermute | solution.py:382
  19.4 0.0 copy-done.1
  19.4 0.0 copy-start.2
  19.4 0.8 %copy-done.2 = f32[16,64,128]{2,1,0:T(8,128)} copy-done((f32[16,64,128]{2,1,0:T(8,128)}, f32[16,64,128]{2,1,0:T(8,128)S(1)}, u32[]{:S(2)}) %copy-start.2) | copy-done | bytes 524312
  20.2 5.1 %first.1 = (f32[16,64,128]{2,1,0:T(8,128)}, f32[16,64,128]{2,1,0:T(8,128)}, f32[8,64,128]{2,1,0:T(8,128)}, f32[8,64,128]{2,1,0:T(8,128)}) custom-call(f32[16,64,128]{2,1,0:T(8,128)} %copy-done.1, f32[16,64,128]{2,1,0:T(8,128)} %copy-done.2, f32[8,64,128]{2,1,0:T(8,128)} %old.1, f32[8,64,128]{2,1,0:T(8,128)} %now.3, f32[8,64,128]{2,1,0:T(8,128)} %vel.1, ...), custom_call_target="tpu_custom_call" | custom-call | tf_op jit(solution)/shard_map/first/pallas_call | solution.py:404
  25.3 0.0 all-to-all-done.got
  25.3 0.0 copy-start.3
  25.3 0.6 %copy-done.3 = f32[16,8,128]{2,1,0:T(8,128)} copy-done((f32[16,8,128]{2,1,0:T(8,128)}, f32[16,8,128]{2,1,0:T(8,128)S(1)}, u32[]{:S(2)}) %copy-start.3) | copy-done | bytes 65560
  25.9 4.8 %second.1 = (f32[8,64,128]{2,1,0:T(8,128)}, f32[8,64,128]{2,1,0:T(8,128)}, f32[8,64,128]{2,1,0:T(8,128)}) custom-call(f32[16,8,128]{2,1,0:T(8,128)} %copy-done.3, f32[9]{0:T(128)} %line_taps.3, f32[16,64,128]{2,1,0:T(8,128)} %get-tuple-element.7.free, f32[16,64,128]{2,1,0:T(8,128)} %get-tuple-element.8.scale, f32[8,64,128]{2,1,0:T(8,128)} %now.3, ...), custom_call_target="tpu_custom_call" | custom-call | tf_op jit(solution)/shard_map/second/pallas_call | solution.py:422
Async XLA Ops:
  0.6 1.2 %copy-start = (f32[8,64,128]{2,1,0:T(8,128)S(1)}, f32[8,64,128]{2,1,0:T(8,128)}, u32[]{:S(2)}) copy-start(f32[8,64,128]{2,1,0:T(8,128)} %now.3) | copy-start | bytes 786436
  2.0 12.2 %collective-permute-start = (f32[16,64,128]{2,1,0:T(8,128)S(1)}, f32[16,64,128]{2,1,0:T(8,128)S(1)}, u32[]{:S(2)}, u32[]{:S(2)}) collective-permute-start(f32[16,64,128]{2,1,0:T(8,128)S(1)} %get-tuple-element.12), channel_id=1, source_target_pairs={{0,1},{1,0},{2,3},{3,2},{4,5},{5,4},{6,7},{7,6},{8,9},{9,8},{10,11... | collective-permute-start | bytes 1572872 | tf_op jit(solution)/shard_map/ppermute | solution.py:381
  2.7 16.7 %collective-permute-start.1 = (f32[16,64,128]{2,1,0:T(8,128)S(1)}, f32[16,64,128]{2,1,0:T(8,128)S(1)}, u32[]{:S(2)}, u32[]{:S(2)}) collective-permute-start(f32[16,64,128]{2,1,0:T(8,128)S(1)} %get-tuple-element.11), channel_id=1, source_target_pairs={{1,2},{3,4},{5,6},{7,8},{9,10},{11,12},{13,14},{2,1},{4,3},{6,5},{... | collective-permute-start | bytes 1572872 | tf_op jit(solution)/shard_map/ppermute | solution.py:382
  8.8 16.5 %all-to-all-start = ((f32[16,8,128]{2,1,0:T(8,128)}), f32[16,8,128]{2,1,0:T(8,128)S(1)}, u32[]{:S(2)}, u32[]{:S(2)}) async-start(f32[16,8,128]{2,1,0:T(8,128)} %pack.1), calls=%async_computation | async-start | bytes 131072 | tf_op jit(solution)/shard_map/all_to_all | solution.py:400
  14.2 5.3 %copy-start.1 = (f32[16,64,128]{2,1,0:T(8,128)}, f32[16,64,128]{2,1,0:T(8,128)S(1)}, u32[]{:S(2)}) copy-start(f32[16,64,128]{2,1,0:T(8,128)S(1)} %collective-permute-done.from_pair) | copy-start | bytes 1572868
  19.4 0.8 %copy-start.2 = (f32[16,64,128]{2,1,0:T(8,128)}, f32[16,64,128]{2,1,0:T(8,128)S(1)}, u32[]{:S(2)}) copy-start(f32[16,64,128]{2,1,0:T(8,128)S(1)} %collective-permute-done.1.from_next) | copy-start | bytes 1572868
  25.3 0.6 %copy-start.3 = (f32[16,8,128]{2,1,0:T(8,128)}, f32[16,8,128]{2,1,0:T(8,128)S(1)}, u32[]{:S(2)}) copy-start(f32[16,8,128]{2,1,0:T(8,128)S(1)} %all-to-all-done.got) | copy-start | bytes 196612

commit v2 on v1

--- a/solution.py
+++ b/solution.py
@@ -17,8 +17,27 @@
 DT_OVER_H = 0.18
 
 VMEM = pl.BlockSpec(memory_space=pltpu.VMEM)
-SMEM = pl.BlockSpec(memory_space=pltpu.SMEM)
+FAR = pl.BlockSpec(memory_space=pltpu.HBM)
+PARAMS = pltpu.CompilerParams(vmem_limit_bytes=16 * 2**20)
 NT_DIMS = (((1,), (1,)), ((), ()))
+
+
+def near(array):
+    return pltpu.with_memory_space_constraint(array, pltpu.VMEM)
+
+
+def far(*arrays):
+    return [pltpu.with_memory_space_constraint(array, pltpu.HBM) for array in arrays]
+
+
+def started(sems, *pairs):
+    copies = [
+        pltpu.make_async_copy(source, target, sems.at[i])
+        for i, (source, target) in enumerate(pairs)
+    ]
+    for copy in copies:
+        copy.start()
+    return copies
 
 
 def parts_of(value, count):
@@ -34,9 +53,90 @@
     return lax.broadcasted_iota(jnp.int32, shape, axis)
 
 
+PAD = 8
+
+
+def laplacian_plane(field, x, size_y):
+    centre = field[x, PAD : PAD + size_y, :]
+    lanes = centre.shape[1]
+    lane = iota(centre.shape, 1)
+    total = 3.0 * COEF[0] * centre
+    for k in range(1, 5):
+        near = field[x + k, PAD : PAD + size_y, :] + field[x - k, PAD : PAD + size_y, :]
+        near = near + field[x, PAD + k : PAD + k + size_y, :]
+        near = near + field[x, PAD - k : PAD - k + size_y, :]
+        near = near + jnp.where(lane < lanes - k, pltpu.roll(centre, lanes - k, 1), 0.0)
+        near = near + jnp.where(lane >= k, pltpu.roll(centre, k, 1), 0.0)
+        total = total + COEF[k] * near
+    return total
+
+
+def own_kernel(names, *refs):
+    old_far, now_far, vel_far = refs[:3]
+    sources = refs[3 : 3 + names]
+    to_pair, to_next = refs[3 + names : 5 + names]
+    targets = refs[5 + names : 5 + 2 * names]
+    old, now, vel, wide, partial, sems = refs[5 + 2 * names :]
+    odd = lax.axis_index("sub") % 2
+    size_x, size_y, lanes = old.shape
+    inside = slice(PAD, PAD + size_y)
+    middle = wide.at[REACH : REACH + size_x, inside, :]
+    copies = started(
+        sems,
+        (now_far, middle),
+        (vel_far, vel),
+        (old_far, old),
+        *zip(sources, targets, strict=True),
+    )
+    planes = wide.shape[0]
+    edge = jnp.zeros((planes, PAD, lanes), jnp.float32)
+    wide[:, 0:PAD, :] = edge
+    wide[:, PAD + size_y :, :] = edge
+    blank = jnp.zeros((REACH, size_y, lanes), jnp.float32)
+    wide[0:REACH, inside, :] = blank
+    wide[REACH + size_x :, inside, :] = blank
+    for copy in copies[:3]:
+        copy.wait()
+
+    def half(target, start):
+        @pl.loop(0, REACH)
+        def _(i):
+            x = start + i
+            own_now = wide[REACH + x, inside, :]
+            speed = vel[x]
+            factor = DT_OVER_H * speed
+            target[i] = own_now
+            target[REACH + i] = (
+                2.0 * own_now
+                - old[x]
+                + factor * factor * laplacian_plane(wide, x + REACH, size_y)
+            )
+            target[2 * REACH + i] = speed
+
+    far = size_x - REACH
+    half(to_next, far * odd)
+    half(to_pair, far * (1 - odd))
+    for copy in copies[3:]:
+        copy.wait()
+
+
 def pack_kernel(
-    devices, cap, block, syn, obs, off, lines, own, cells, taps, line_taps, send
+    devices,
+    cap,
+    block,
+    line_taps_far,
+    syn,
+    obs,
+    off,
+    lines,
+    own,
+    cells,
+    taps,
+    send,
+    line_taps,
+    sems,
 ):
+    copies = started(sems, (line_taps_far, line_taps))
     me = lax.axis_index("sub")
     count, samples = syn.shape
     ntap = taps.shape[1]
@@ -64,6 +164,7 @@
     before = lines[0:1, :]
     after = lines[1:2, :]
     sources = jnp.zeros((8, count), jnp.float32)
+    copies[0].wait()
     for reach in range(-SW, SW + 1):
         term = line_taps[reach + SW] * (
             pltpu.roll(both, (-reach) % count, 1) if reach else both
@@ -133,70 +234,38 @@
     send[:, 7, :] = jnp.broadcast_to(edge[9:10], shape)
 
 
-PAD = 8
-
-
-def laplacian_plane(field, x, size_y):
-    centre = field[x, PAD : PAD + size_y, :]
-    lanes = centre.shape[1]
-    lane = iota(centre.shape, 1)
-    total = 3.0 * COEF[0] * centre
-    for k in range(1, 5):
-        near = field[x + k, PAD : PAD + size_y, :] + field[x - k, PAD : PAD + size_y, :]
-        near = near + field[x, PAD + k : PAD + k + size_y, :]
-        near = near + field[x, PAD - k : PAD - k + size_y, :]
-        near = near + jnp.where(lane < lanes - k, pltpu.roll(centre, lanes - k, 1), 0.0)
-        near = near + jnp.where(lane >= k, pltpu.roll(centre, k, 1), 0.0)
-        total = total + COEF[k] * near
-    return total
-
-
-def first_kernel(
-    from_pair, from_next, old, now, vel, fwd, free, scale, weight0, weight1, wide, edges
-):
-    odd = lax.axis_index("sub") % 2
+def squared(speed):
+    factor = DT_OVER_H * speed
+    return factor * factor
+
+
+def inner_kernel(old_far, now_far, vel_far, fwd_far, partial, weight0, weight1, wide, old, vel, fwd, sems):
     size_x, size_y, lanes = old.shape
-    zeros = jnp.zeros((wide.shape[0], PAD, lanes), jnp.float32)
-    wide[:, 0:PAD, :] = zeros
-    wide[:, PAD + size_y :, :] = zeros
     inside = slice(PAD, PAD + size_y)
-    wide[2 * REACH : 2 * REACH + size_x, inside, :] = now[...]
-    above = 2 * REACH + size_x
-
-    def place(lower, upper):
-        wide[0 : 2 * REACH, inside, :] = lower[0 : 2 * REACH]
-        wide[above : above + 2 * REACH, inside, :] = upper[0 : 2 * REACH]
-        edges[0] = lower[2 * REACH : 3 * REACH]
-        edges[1] = lower[3 * REACH : 4 * REACH]
-        edges[2] = upper[2 * REACH : 3 * REACH]
-        edges[3] = upper[3 * REACH : 4 * REACH]
-
-    @pl.when(odd == 0)
-    def _():
-        place(from_next, from_pair)
-
-    @pl.when(odd == 1)
-    def _():
-        place(from_pair, from_next)
-
-    def step(out_x, older, speed):
-        factor = DT_OVER_H * speed
-        factor = factor * factor
-        scale[out_x] = factor
-        x = out_x + REACH
-        free[out_x] = (
-            2.0 * wide[x, inside, :] - older + factor * laplacian_plane(wide, x, size_y)
-        )
-
-    @pl.loop(0, REACH)
-    def _(x):
-        step(x, edges[0, x], edges[1, x])
-        step(x + REACH + size_x, edges[2, x], edges[3, x])
+    copies = started(
+        sems,
+        (now_far, wide.at[REACH : REACH + size_x, inside, :]),
+        (vel_far, vel),
+        (old_far, old),
+        (fwd_far, fwd),
+    )
+    edge = jnp.zeros((wide.shape[0], PAD, lanes), jnp.float32)
+    wide[:, 0:PAD, :] = edge
+    wide[:, PAD + size_y :, :] = edge
+    blank = jnp.zeros((REACH, size_y, lanes), jnp.float32)
+    wide[0:REACH, inside, :] = blank
+    wide[REACH + size_x :, inside, :] = blank
+    for copy in copies:
+        copy.wait()
 
     @pl.loop(0, size_x)
     def _(x):
         speed = vel[x]
-        step(x + REACH, old[x], speed)
+        partial[x] = (
+            2.0 * wide[REACH + x, inside, :]
+            - old[x]
+            + squared(speed) * laplacian_plane(wide, x + REACH, size_y)
+        )
         weight = 2.0 / (speed * speed * speed)
         f1 = fwd[1, x]
         f2 = fwd[2, x]
@@ -204,22 +273,80 @@
         weight1[x] = weight * (f1 - 2.0 * f2 + fwd[3, x])
 
 
+def across(field, x, low, high):
+    total = None
+    for k in range(1, 5):
+        for at in (x - k, x + k):
+            if low <= at < high:
+                term = COEF[k] * field[at - low]
+                total = term if total is None else total + term
+    return total
+
+
+def first_kernel(
+    from_pair, from_next, partial, now, vel, free, scale
+):
+    odd = lax.axis_index("sub") % 2
+    size_x = now.shape[0]
+    top = REACH + size_x
+
+    def border(source, first_out, low):
+        for i in range(REACH):
+            factor = squared(source[2 * REACH + i])
+            scale[first_out + i] = factor
+            free[first_out + i] = source[REACH + i] + factor * across(now, low + i, 0, size_x)
+        planes = range(REACH) if low < 0 else range(size_x - REACH, size_x)
+        for x in planes:
+            factor = squared(vel[x])
+            scale[REACH + x] = factor
+            free[REACH + x] = partial[x] + factor * across(source, x, low, low + REACH)
+
+    @pl.when(odd == 0)
+    def _():
+        border(from_next, 0, -REACH)
+        border(from_pair, top, size_x)
+
+    @pl.when(odd == 1)
+    def _():
+        border(from_pair, 0, -REACH)
+        border(from_next, top, size_x)
+
+
 def second_kernel(
     devices,
     cap,
     got,
+    line_taps_far,
+    free_far,
+    scale_far,
+    now_far,
+    weight0_far,
+    weight1_far,
+    prior_far,
+    last_far,
+    gradient_far,
     line_taps,
     free,
     scale,
     now,
     weight0,
     weight1,
-    prior,
     last,
     gradient,
     field,
     source1,
+    sems,
+    out_sems,
 ):
+    copies = started(
+        sems,
+        (line_taps_far, line_taps),
+        (free_far, free),
+        (scale_far, scale),
+        (now_far, now),
+        (weight0_far, weight0),
+        (weight1_far, weight1),
+    )
     me = lax.axis_index("sub")
     size_x, size_y, lanes = now.shape
     rows = size_x * size_y
@@ -241,6 +368,7 @@
     e = spot % EDGE
     count = edge[7:8]
     missing = jnp.zeros((8, width), jnp.float32)
+    copies[0].wait()
     for reach in range(-SW, SW + 1):
         if reach == 0:
             continue
@@ -313,14 +441,19 @@
     inside = slice(PAD, PAD + size_y)
     top = REACH + size_x
 
+    for copy in copies[1:]:
+        copy.wait()
     out = inject(own_a, own_b)
     first = (out[:, 0:lanes] + out[:, lanes : 2 * lanes]).reshape(size_x, size_y, lanes)
     source1[...] = (out[:, 2 * lanes : 3 * lanes] + out[:, 3 * lanes :]).reshape(
         size_x, size_y, lanes
     )
     fresh = free[REACH:top] + scale[REACH:top] * first
-    prior[...] = fresh
     field[REACH:top, inside, :] = fresh
+    done = [
+        pltpu.make_async_copy(field.at[REACH:top, inside, :], prior_far, out_sems.at[0])
+    ]
+    done[0].start()
     out = inject(low_a, low_b)
     first = (out[:, 0:lanes] + out[:, lanes:]).reshape(REACH, size_y, lanes)
     field[0:REACH, inside, :] = free[0:REACH] + scale[0:REACH] * first
@@ -328,17 +461,29 @@
     first = (out[:, 0:lanes] + out[:, lanes:]).reshape(REACH, size_y, lanes)
     field[top:, inside, :] = free[top:] + scale[top:] * first
 
-    @pl.loop(0, size_x)
-    def _(x):
-        at = x + REACH
-        fresh = field[at, inside, :]
-        following = (
-            2.0 * fresh
-            - now[x]
-            + scale[at] * (laplacian_plane(field, at, size_y) + source1[x])
+    half = size_x // 2
+    for part in range(2):
+        planes = slice(part * half, (part + 1) * half)
+
+        @pl.loop(part * half, (part + 1) * half)
+        def _(x):
+            at = x + REACH
+            fresh = field[at, inside, :]
+            following = (
+                2.0 * fresh
+                - now[x]
+                + scale[at] * (laplacian_plane(field, at, size_y) + source1[x])
+            )
+            last[x] = following
+            gradient[x] = weight0[x] * fresh + weight1[x] * following
+
+        done += started(
+            out_sems.at[pl.ds(1 + 2 * part, 2)],
+            (last.at[planes], last_far.at[planes]),
+            (gradient.at[planes], gradient_far.at[planes]),
         )
-        last[x] = following
-        gradient[x] = weight0[x] * fresh + weight1[x] * following
+    for copy in done:
+        copy.wait()
 
 
 def body(
@@ -358,7 +503,6 @@
     count = synthetic.shape[0]
     size_x, size_y, lanes = velocity.shape
     devices = lax.axis_size("sub")
-    me = lax.axis_index("sub")
     cap = max(2, 2 * count // devices)
     f32 = jnp.float32
 
@@ -366,70 +510,90 @@
     following = [(i, i + 1) for i in range(1, devices - 1, 2)]
     following = following + [(b, a) for a, b in following]
 
-    def edge_planes(start):
-        return jnp.concatenate(
-            [
-                adjoint_now,
-                lax.dynamic_slice_in_dim(adjoint_old, start, REACH, 0),
-                lax.dynamic_slice_in_dim(velocity, start, REACH, 0),
-            ],
-            axis=0,
-        )
-
-    odd = me % 2
-    top = size_x - REACH
-    from_pair = lax.ppermute(edge_planes(jnp.where(odd == 0, top, 0)), "sub", pair)
-    from_next = lax.ppermute(edge_planes(jnp.where(odd == 0, 0, top)), "sub", following)
+    plane = (size_y, lanes)
+    outer = size_x + 2 * REACH
+    inner = pltpu.VMEM((size_x,) + plane, f32)
+    padded = pltpu.VMEM((outer, size_y + 2 * PAD, lanes), f32)
+    halo = pltpu.VMEM((3 * REACH,) + plane, f32)
+    wider = pltpu.VMEM((outer,) + plane, f32)
+    inner_far = pltpu.HBM((size_x,) + plane, f32)
+    wider_far = pltpu.HBM((outer,) + plane, f32)
+    dma = pltpu.SemaphoreType.DMA
+
+    row = (1, count)
+    traces = (
+        synthetic,
+        observed,
+        offsets.reshape(row),
+        lines,
+        owners.reshape(row),
+        cells.reshape(row),
+        taps.reshape(1, -1),
+    )
+    to_pair, to_next, *traces = pl.pallas_call(
+        functools.partial(own_kernel, len(traces)),
+        out_shape=(halo, halo) + tuple(pltpu.VMEM(t.shape, t.dtype) for t in traces),
+        in_specs=[FAR] * (3 + len(traces)),
+        out_specs=(VMEM,) * (2 + len(traces)),
+        scratch_shapes=[inner, inner, inner, padded, inner, dma((3 + len(traces),))],
+        compiler_params=PARAMS,
+        name="own",
+    )(*far(adjoint_old, adjoint_now, velocity, *traces))
+    from_next = lax.ppermute(to_next, "sub", following)
+    from_pair = lax.ppermute(to_pair, "sub", pair)
 
     send = pl.pallas_call(
         functools.partial(pack_kernel, devices, cap, velocity.size),
         out_shape=jax.ShapeDtypeStruct((devices, 8, LANES), f32),
-        in_specs=[VMEM] * 7 + [SMEM],
+        in_specs=[FAR] + [VMEM] * len(traces),
         out_specs=VMEM,
+        scratch_shapes=[pltpu.SMEM(line_taps.shape, f32), dma((1,))],
+        compiler_params=PARAMS,
         name="pack",
-    )(
-        synthetic,
-        observed,
-        offsets.reshape(1, count),
-        lines,
-        owners.reshape(1, count),
-        cells.reshape(1, count),
-        taps.reshape(1, -1),
-        line_taps,
-    )
+    )(*far(line_taps), *(near(t) for t in traces))
     got = lax.all_to_all(send, "sub", split_axis=0, concat_axis=0, tiled=True)
 
-    plane = (size_y, lanes)
-    outer = size_x + 2 * REACH
-    free, scale, weight0, weight1 = pl.pallas_call(
+    partial, weight0, weight1 = pl.pallas_call(
+        inner_kernel,
+        out_shape=(inner_far,) * 3,
+        in_specs=[FAR] * 4,
+        out_specs=(VMEM,) * 3,
+        scratch_shapes=[padded, inner, inner, pltpu.VMEM(forward.shape, f32), dma((4,))],
+        compiler_params=PARAMS,
+        name="inner",
+    )(*far(adjoint_old, adjoint_now, velocity, forward))
+    free, scale = pl.pallas_call(
         first_kernel,
-        out_shape=(
-            jax.ShapeDtypeStruct((outer,) + plane, f32),
-            jax.ShapeDtypeStruct((outer,) + plane, f32),
-            jax.ShapeDtypeStruct((size_x,) + plane, f32),
-            jax.ShapeDtypeStruct((size_x,) + plane, f32),
-        ),
-        in_specs=[VMEM] * 6,
-        out_specs=(VMEM,) * 4,
-        scratch_shapes=[
-            pltpu.VMEM((size_x + 4 * REACH, size_y + 2 * PAD, lanes), f32),
-            pltpu.VMEM((4, REACH) + plane, f32),
-        ],
+        out_shape=(wider_far,) * 2,
+        in_specs=[VMEM] * 5,
+        out_specs=(VMEM,) * 2,
+        compiler_params=PARAMS,
         name="first",
-    )(from_pair, from_next, adjoint_old, adjoint_now, velocity, forward)
+    )(near(from_pair), near(from_next), *far(partial, adjoint_now, velocity))
 
     field = jax.ShapeDtypeStruct((size_x,) + plane, f32)
     return pl.pallas_call(
         functools.partial(second_kernel, devices, cap),
         out_shape=(field, field, field),
-        in_specs=[VMEM, SMEM] + [VMEM] * 5,
-        out_specs=(VMEM,) * 3,
+        in_specs=[VMEM] + [FAR] * 6,
+        out_specs=(FAR,) * 3,
         scratch_shapes=[
+            pltpu.SMEM(line_taps.shape, f32),
+            wider,
+            wider,
+            inner,
+            inner,
+            inner,
+            inner,
+            inner,
             pltpu.VMEM((outer, size_y + 2 * PAD, lanes), f32),
-            pltpu.VMEM((size_x,) + plane, f32),
+            inner,
+            dma((6,)),
+            dma((5,)),
         ],
+        compiler_params=PARAMS,
         name="second",
-    )(got, line_taps, free, scale, adjoint_now, weight0, weight1)
+    )(near(got), *far(line_taps, free, scale, adjoint_now, weight0, weight1))
 
 
 def solution(mesh):

time: 31 us -> 26.8 us (0.86)
  the two profiles are of different devices: /device:TPU:9 before, /device:TPU:0 now
where the time goes in v2:
time: 26.8 us; the launch traced here: 26.5 us
  Pallas kernels  14.6 us (54%)
  starting transfers between devices  9.98 us (37%)
  waiting for transfers between devices  1.16 us (4%)
  between operations  0.69 us (3%)
    all_to_all x1, starting transfers between devices, body(): got = lax.all_to_all(send, 'sub', split_axis=0, concat_axis=0, tiled=True)  8.79 us
    pallas_call x1, Pallas kernels, body(): pl.pallas_call(functools.partial(second_kernel, devices, cap), out_shape=...  4.71 us
    pallas_call x1, Pallas kernels, body(): pl.pallas_call(inner_kernel, out_shape=(inner_far,) * 3, in_specs=[FAR] *...  3.48 us
    pallas_call x1, Pallas kernels, body(): pl.pallas_call(functools.partial(own_kernel, len(traces)), out_shape=(hal...  2.37 us
    pallas_call x1, Pallas kernels, body(): pl.pallas_call(first_kernel, out_shape=(wider_far,) * 2, in_specs=[VMEM]...  2.24 us
    pallas_call x1, Pallas kernels, body(): pl.pallas_call(functools.partial(pack_kernel, devices, cap, velocity.size...  1.85 us
    all_to_all x1, waiting for transfers between devices, body(): got = lax.all_to_all(send, 'sub', split_axis=0, concat_axis=0, tiled=True)  1.15 us
    ppermute x1, starting transfers between devices, body(): from_next = lax.ppermute(to_next, 'sub', following)  0.67 us
  transfers between devices with their start and end apart: 3, of which 1 were waited for; matrix products, arithmetic and copies ran while one was open for 0% of the time, Pallas kernels for 29%

profile of v2, /device:TPU:0, one launch (start us, length us, event | category | flops | bytes accessed | tf_op | source)
XLA Modules:
  0.0 26.5 jit_solution(14557705427834399871)
XLA Ops:
  0.6 2.4 %own.1 = (f32[12,64,128]{2,1,0:T(8,128)S(1)}, f32[12,64,128]{2,1,0:T(8,128)S(1)}, f32[512,256]{1,0:T(8,128)S(1)}, f32[512,256]{1,0:T(8,128)S(1)}, s32[1,512]{1,0...) custom-call(f32[8,64,128]{2,1,0:T(8,128)} %old_far.1, ...), custom_call_target="tpu_custom_call" | custom-call | tf_op jit(solution)/shard_map/own/pallas_call | solution.py:533
  3.0 0.5 %collective-permute-start = (f32[12,64,128]{2,1,0:T(8,128)S(1)}, f32[12,64,128]{2,1,0:T(8,128)S(1)}, u32[]{:S(2)}, u32[]{:S(2)}) collective-permute-start(f32[12,64,128]{2,1,0:T(8,128)S(1)} %get-tuple-element.24), channel_id=1, source_target_pairs={{0,1},{1,0},{2,3},{3,2},{4,5},{5,4},{6,7},{7,6},{8,9},{9,8},{10,11... | collective-permute-start | bytes 1179656 | tf_op jit(solution)/shard_map/ppermute | solution.py:543
  3.5 0.7 %collective-permute-start.1 = (f32[12,64,128]{2,1,0:T(8,128)S(1)}, f32[12,64,128]{2,1,0:T(8,128)S(1)}, u32[]{:S(2)}, u32[]{:S(2)}) collective-permute-start(f32[12,64,128]{2,1,0:T(8,128)S(1)} %get-tuple-element.25), channel_id=1, source_target_pairs={{1,2},{3,4},{5,6},{7,8},{9,10},{11,12},{13,14},{2,1},{4,3},{6,5},{... | collective-permute-start | bytes 1179656 | tf_op jit(solution)/shard_map/ppermute | solution.py:542
  4.2 1.9 %pack.1 = f32[16,8,128]{2,1,0:T(8,128)} custom-call(f32[9]{0:T(128)} %line_taps_far.3, f32[512,256]{1,0:T(8,128)S(1)} %get-tuple-element.17.syn, f32[512,256]{1,0:T(8,128)S(1)} %get-tuple-element.18.obs, s32[1,512]{1,0:T(1,128)S(1)} %get-tuple-element.19.off, s32[2,512]{1,0:T(2,128)S(1)} %get-tuple-element.20.lines, s32[1,512]{1,0:T(1,128)S(1)} %get-tuple-element.21.own, ...), custom_call_target="tpu_custom_call" | custom-call | tf_op jit(solution)/shard_map/pack/pallas_call | solution.py:545
  6.1 8.8 %all-to-all-start = ((f32[16,8,128]{2,1,0:T(8,128)}), f32[16,8,128]{2,1,0:T(8,128)S(1)}, u32[]{:S(2)}, u32[]{:S(2)}) async-start(f32[16,8,128]{2,1,0:T(8,128)} %pack.1), calls=%async_computation | async-start | bytes 131072 | tf_op jit(solution)/shard_map/all_to_all | solution.py:554
  14.9 3.5 %inner.1 = (f32[8,64,128]{2,1,0:T(8,128)}, f32[8,64,128]{2,1,0:T(8,128)}, f32[8,64,128]{2,1,0:T(8,128)}) custom-call(f32[8,64,128]{2,1,0:T(8,128)} %old_far.1, f32[8,64,128]{2,1,0:T(8,128)} %now_far.3, f32[8,64,128]{2,1,0:T(8,128)} %vel.1, f32[4,8,64,128]{3,2,1,0:T(8,128)} %fwd_far.1), custom_call_target="tpu_custom_call" | custom-call | tf_op jit(solution)/shard_map/inner/pallas_call | solution.py:556
  18.4 0.0 collective-permute-done.from_pair
  18.4 0.0 collective-permute-done.1.from_next
  18.4 2.2 %first.1 = (f32[16,64,128]{2,1,0:T(8,128)}, f32[16,64,128]{2,1,0:T(8,128)}) custom-call(f32[12,64,128]{2,1,0:T(8,128)S(1)} %collective-permute-done.from_pair, f32[12,64,128]{2,1,0:T(8,128)S(1)} %collective-permute-done.1.from_next, f32[8,64,128]{2,1,0:T(8,128)} %get-tuple-element.26.partial, f32[8,64,128]{2,1,0:T(8,128)} %now_far.3, f32[8,64,128]{2,1,0:T(8,128)} %vel.1), custom_call_target="tpu_custom_call" | custom-call | tf_op jit(solution)/shard_map/first/pallas_call | solution.py:565
  20.6 1.2 %all-to-all-done.got = f32[16,8,128]{2,1,0:T(8,128)S(1)} async-done(((f32[16,8,128]{2,1,0:T(8,128)}), f32[16,8,128]{2,1,0:T(8,128)S(1)}, u32[]{:S(2)}, u32[]{:S(2)}) %all-to-all-start) | async-done | bytes 65568 | tf_op jit(solution)/shard_map/all_to_all | solution.py:554
  21.8 4.7 %second.1 = (f32[8,64,128]{2,1,0:T(8,128)}, f32[8,64,128]{2,1,0:T(8,128)}, f32[8,64,128]{2,1,0:T(8,128)}) custom-call(f32[16,8,128]{2,1,0:T(8,128)S(1)} %all-to-all-done.got, f32[9]{0:T(128)} %line_taps_far.3, f32[16,64,128]{2,1,0:T(8,128)} %get-tuple-element.27.free_far, f32[16,64,128]{2,1,0:T(8,128)} %get-tuple-element.28.scale_far, ...), custom_call_target="tpu_custom_call" | custom-call | tf_op jit(solution)/shard_map/second/pallas_call | solution.py:575
Async XLA Ops:
  3.0 15.3 %collective-permute-start = (f32[12,64,128]{2,1,0:T(8,128)S(1)}, f32[12,64,128]{2,1,0:T(8,128)S(1)}, u32[]{:S(2)}, u32[]{:S(2)}) collective-permute-start(f32[12,64,128]{2,1,0:T(8,128)S(1)} %get-tuple-element.24), channel_id=1, source_target_pairs={{0,1},{1,0},{2,3},{3,2},{4,5},{5,4},{6,7},{7,6},{8,9},{9,8},{10,11... | collective-permute-start | bytes 1179656 | tf_op jit(solution)/shard_map/ppermute | solution.py:543
  3.5 14.8 %collective-permute-start.1 = (f32[12,64,128]{2,1,0:T(8,128)S(1)}, f32[12,64,128]{2,1,0:T(8,128)S(1)}, u32[]{:S(2)}, u32[]{:S(2)}) collective-permute-start(f32[12,64,128]{2,1,0:T(8,128)S(1)} %get-tuple-element.25), channel_id=1, source_target_pairs={{1,2},{3,4},{5,6},{7,8},{9,10},{11,12},{13,14},{2,1},{4,3},{6,5},{... | collective-permute-start | bytes 1179656 | tf_op jit(solution)/shard_map/ppermute | solution.py:542
  6.1 15.7 %all-to-all-start = ((f32[16,8,128]{2,1,0:T(8,128)}), f32[16,8,128]{2,1,0:T(8,128)S(1)}, u32[]{:S(2)}, u32[]{:S(2)}) async-start(f32[16,8,128]{2,1,0:T(8,128)} %pack.1), calls=%async_computation | async-start | bytes 131072 | tf_op jit(solution)/shard_map/all_to_all | solution.py:554

commit v3 on v2

v3 whole, which is shorter than its diff:
```python
import functools

import jax
import jax.numpy as jnp
from jax import lax
from jax.experimental import pallas as pl
from jax.experimental.pallas import tpu as pltpu
from jax.sharding import PartitionSpec as P

SW = 4
STEPS = 2
REACH = 4
LANES = 128
EDGE = 2 * SW

COEF = (-205.0 / 72.0, 8.0 / 5.0, -1.0 / 5.0, 8.0 / 315.0, -1.0 / 560.0)
DT_OVER_H = 0.18

VMEM = pl.BlockSpec(memory_space=pltpu.VMEM)
FAR = pl.BlockSpec(memory_space=pltpu.HBM)
PARAMS = pltpu.CompilerParams(vmem_limit_bytes=16 * 2**20)
NT_DIMS = (((1,), (1,)), ((), ()))


def near(array):
    return pltpu.with_memory_space_constraint(array, pltpu.VMEM)


def far(*arrays):
    return [pltpu.with_memory_space_constraint(array, pltpu.HBM) for array in arrays]


def started(sems, *pairs):
    copies = [
        pltpu.make_async_copy(source, target, sems.at[i])
        for i, (source, target) in enumerate(pairs)
    ]
    for copy in copies:
        copy.start()
    return copies


def parts_of(value, count):
    parts = []
    for _ in range(count):
        part = value.astype(jnp.bfloat16).astype(jnp.float32)
        parts.append(part)
        value = value - part
    return parts


def iota(shape, axis):
    return lax.broadcasted_iota(jnp.int32, shape, axis)


PACKED = 16


def across16(row):
    return jnp.broadcast_to(row, (PACKED, row.shape[1])).astype(jnp.int16)[None]


def index16(count, width):
    rows = iota((count, width), 0).astype(jnp.int16)
    return rows.reshape(count // PACKED, PACKED, width)


def same16(index, row):
    return index == across16(row)


def pick16(mask, row):
    width = row.shape[1]
    wide = jnp.broadcast_to(row, (PACKED, width)).astype(jnp.bfloat16)
    picked = jnp.where(mask, wide[None], jnp.zeros((), jnp.bfloat16))
    return picked.reshape(-1, width)


def hot16(index, row):
    return pick16(same16(index, row), jnp.ones(row.shape, jnp.float32))


PAD = 8


def laplacian_plane(field, x, size_y):
    centre = field[x, PAD : PAD + size_y, :]
    lanes = centre.shape[1]
    lane = iota(centre.shape, 1)
    total = 3.0 * COEF[0] * centre
    for k in range(1, 5):
        near = field[x + k, PAD : PAD + size_y, :] + field[x - k, PAD : PAD + size_y, :]
        near = near + field[x, PAD + k : PAD + k + size_y, :]
        near = near + field[x, PAD - k : PAD - k + size_y, :]
        near = near + jnp.where(lane < lanes - k, pltpu.roll(centre, lanes - k, 1), 0.0)
        near = near + jnp.where(lane >= k, pltpu.roll(centre, k, 1), 0.0)
        total = total + COEF[k] * near
    return total


def squared(speed):
    factor = DT_OVER_H * speed
    return factor * factor


def send_kernel(
    devices,
    cap,
    block,
    own_far,
    cells_far,
    taps_far,
    off_far,
    lines_far,
    line_taps_far,
    syn_far,
    obs_far,
    now_far,
    vel_far,
    old_far,
    send_far,
    to_pair,
    to_next,
    own,
    cells,
    taps,
    off,
    lines,
    line_taps,
    syn,
    obs,
    old,
    vel,
    wide,
    send,
    sems,
):
    size_x, size_y, lanes = old.shape
    inside = slice(PAD, PAD + size_y)
    copies = started(
        sems,
        (own_far, own),
        (cells_far, cells),
        (taps_far, taps),
        (off_far, off),
        (lines_far, lines),
        (line_taps_far, line_taps),
        (syn_far, syn),
        (obs_far, obs),
        (now_far, wide.at[REACH : REACH + size_x, inside, :]),
        (vel_far, vel),
        (old_far, old),
    )
    edge = jnp.zeros((wide.shape[0], PAD, lanes), jnp.float32)
    wide[:, 0:PAD, :] = edge
    wide[:, PAD + size_y :, :] = edge
    blank = jnp.zeros((REACH, size_y, lanes), jnp.float32)
    wide[0:REACH, inside, :] = blank
    wide[REACH + size_x :, inside, :] = blank
    for copy in copies[:6]:
        copy.wait()
    me = lax.axis_index("sub")
    count, samples = syn.shape
    ntap = taps.shape[1]
    pack = LANES // cap
    group = LANES // EDGE
    place = iota((1, count), 1)
    owner = own[...]
    owned = same16(index16(devices, count), owner)
    one_hot = pick16(owned, jnp.ones((1, count), jnp.float32))
    chunks = [one_hot[:, at : at + LANES] for at in range(0, count, LANES)]
    ahead = index16(LANES, LANES) < across16(iota((1, LANES), 1))
    ranks = jnp.dot(
        jnp.concatenate(chunks, axis=0),
        pick16(ahead, jnp.ones((1, LANES), jnp.float32)),
        preferred_element_type=jnp.float32,
    )
    base = jnp.zeros((devices, 1), jnp.float32)
    rank = []
    for i, chunk in enumerate(chunks):
        chunk = chunk.astype(jnp.float32)
        rank.append(
            jnp.sum(
                chunk * (ranks[i * devices : (i + 1) * devices] + base), axis=0, keepdims=True
            )
        )
        base = base + jnp.sum(chunk, axis=1, keepdims=True)
    rank = jnp.concatenate(rank, axis=1).astype(jnp.int32)
    lane = index16(LANES, count)
    slot = hot16(lane, rank + (me % pack) * cap)
    edge_lane = jnp.where(
        place < SW, place, jnp.where(place >= count - SW, place - count + EDGE, -LANES)
    )
    chosen = hot16(lane, edge_lane + (me % group) * EDGE)

    row = jnp.concatenate([taps[...], jnp.zeros((1, samples - ntap), jnp.float32)], axis=1)
    starts = -(-(samples - ntap + 1) // 8) * 8
    toeplitz = pltpu.roll(
        jnp.broadcast_to(row, (starts, samples)), 0, 1, stride=1, stride_axis=0
    )
    for copy in copies[6:8]:
        copy.wait()
    all_starts = lax.dot_general(
        toeplitz,
        syn[...] - obs[...],
        NT_DIMS,
        precision=lax.Precision.HIGHEST,
        preferred_element_type=jnp.float32,
    )
    start = iota((starts, count), 0)
    offset = off[...]
    filtered = [
        jnp.sum(jnp.where(start == offset + step, all_starts, 0.0), axis=0, keepdims=True)
        for step in range(STEPS)
    ]
    both = jnp.concatenate(filtered + [jnp.zeros((8 - STEPS, count), jnp.float32)], axis=0)
    before = lines[0:1, :]
    after = lines[1:2, :]
    sources = jnp.zeros((8, count), jnp.float32)
    for reach in range(-SW, SW + 1):
        term = line_taps[0:1, reach + SW : reach + SW + 1] * (
            pltpu.roll(both, (-reach) % count, 1) if reach else both
        )
        if reach < 0:
            keep = (before >= -reach) & (place >= -reach)
        elif reach > 0:
            keep = (after >= reach) & (place < count - reach)
        else:
            keep = before >= 0
        sources = sources + jnp.where(keep, term, 0.0)
    cell = cells[...]
    high = (cell >> 8).astype(jnp.float32)
    low = (cell & 255).astype(jnp.float32)
    pieces = parts_of(sources[0:1], 3) + parts_of(sources[1:2], 3) + [high, low]
    spread = jnp.concatenate([pick16(owned, piece) for piece in pieces], axis=0)
    out = lax.dot_general(spread, slot, NT_DIMS, preferred_element_type=jnp.float32)
    part = [out[k * devices : (k + 1) * devices] for k in range(8)]
    value0 = part[0] + part[1] + part[2]
    value1 = part[3] + part[4] + part[5]
    where = 256.0 * part[6] + part[7]
    none = jnp.zeros((1, LANES), jnp.float32)

    def to_upper(rows):
        return pltpu.roll(jnp.concatenate([none, rows[:-1]], axis=0), LANES // 2, 1)

    def to_lower(rows):
        return pltpu.roll(jnp.concatenate([rows[1:], none], axis=0), LANES // 2, 1)

    send[:, 0, :] = value0 + to_upper(value0)
    send[:, 1, :] = where + to_upper(where)
    send[:, 2, :] = value1 + to_lower(value0)
    send[:, 3, :] = to_lower(where)
    count_ = jnp.where(place < SW, before, after).astype(jnp.float32)
    edge_rows = (
        parts_of(both[0:1], 3)
        + parts_of(both[1:2], 3)
        + [owner.astype(jnp.float32), high, low, count_]
    )
    edge_rows = jnp.concatenate(
        edge_rows + [jnp.zeros((16 - len(edge_rows), count), jnp.float32)], axis=0
    ).astype(jnp.bfloat16)
    edge = lax.dot_general(edge_rows, chosen, NT_DIMS, preferred_element_type=jnp.float32)
    edge_cell = edge[6:7] * float(block) + 256.0 * edge[7:8] + edge[8:9]
    shape = (devices, LANES)
    send[:, 4, :] = jnp.broadcast_to(edge[0:1] + edge[1:2] + edge[2:3], shape)
    send[:, 5, :] = jnp.broadcast_to(edge[3:4] + edge[4:5] + edge[5:6], shape)
    send[:, 6, :] = jnp.broadcast_to(edge_cell, shape)
    send[:, 7, :] = jnp.broadcast_to(edge[9:10], shape)
    sent = pltpu.make_async_copy(send, send_far, sems.at[11])
    sent.start()
    for copy in copies[8:]:
        copy.wait()
    odd = me % 2

    def half(target, start):
        for i in range(REACH):
            x = start + i
            own_now = wide[REACH + x, inside, :]
            speed = vel[x]
            target[i] = own_now
            target[REACH + i] = (
                2.0 * own_now
                - old[x]
                + squared(speed) * laplacian_plane(wide, x + REACH, size_y)
            )
            target[2 * REACH + i] = speed

    far_half = size_x - REACH
    half(to_next, far_half * odd)
    half(to_pair, far_half * (1 - odd))
    sent.wait()


def inner_kernel(old_far, now_far, vel_far, fwd_far, partial, now, vel, weight0, weight1, wide, old, fwd, sems):
    size_x, size_y, lanes = old.shape
    inside = slice(PAD, PAD + size_y)
    copies = started(
        sems,
        (now_far, wide.at[REACH : REACH + size_x, inside, :]),
        (vel_far, vel),
        (old_far, old),
        (fwd_far, fwd),
    )
    edge = jnp.zeros((wide.shape[0], PAD, lanes), jnp.float32)
    wide[:, 0:PAD, :] = edge
    wide[:, PAD + size_y :, :] = edge
    blank = jnp.zeros((REACH, size_y, lanes), jnp.float32)
    wide[0:REACH, inside, :] = blank
    wide[REACH + size_x :, inside, :] = blank
    for copy in copies:
        copy.wait()

    for x in range(size_x):
        speed = vel[x]
        now[x] = wide[REACH + x, inside, :]
        partial[x] = (
            2.0 * now[x]
            - old[x]
            + squared(speed) * laplacian_plane(wide, x + REACH, size_y)
        )
        weight = 2.0 / (speed * speed * speed)
        f1 = fwd[1, x]
        f2 = fwd[2, x]
        weight0[x] = weight * (fwd[0, x] - 2.0 * f1 + f2)
        weight1[x] = weight * (f1 - 2.0 * f2 + fwd[3, x])


def across(field, x, low, high):
    total = None
    for k in range(1, 5):
        for at in (x - k, x + k):
            if low <= at < high:
                term = COEF[k] * field[at - low]
                total = term if total is None else total + term
    return total


def first_kernel(
    from_pair, from_next, partial, now, vel, free, scale
):
    odd = lax.axis_index("sub") % 2
    size_x = now.shape[0]
    top = REACH + size_x

    def border(source, first_out, low):
        for i in range(REACH):
            factor = squared(source[2 * REACH + i])
            scale[first_out + i] = factor
            free[first_out + i] = source[REACH + i] + factor * across(now, low + i, 0, size_x)
        planes = range(REACH) if low < 0 else range(size_x - REACH, size_x)
        for x in planes:
            factor = squared(vel[x])
            scale[REACH + x] = factor
            free[REACH + x] = partial[x] + factor * across(source, x, low, low + REACH)

    @pl.when(odd == 0)
    def _():
        border(from_next, 0, -REACH)
        border(from_pair, top, size_x)

    @pl.when(odd == 1)
    def _():
        border(from_pair, 0, -REACH)
        border(from_next, top, size_x)


def second_kernel(
    devices,
    cap,
    got,
    free,
    scale,
    line_taps_far,
    now_far,
    weight0_far,
    weight1_far,
    prior_far,
    last_far,
    gradient_far,
    line_taps,
    now,
    weight0,
    weight1,
    last,
    gradient,
    field,
    source1,
    sems,
    out_sems,
):
    copies = started(
        sems,
        (line_taps_far, line_taps),
        (now_far, now),
        (weight0_far, weight0),
        (weight1_far, weight1),
    )
    me = lax.axis_index("sub")
    size_x, size_y, lanes = now.shape
    rows = size_x * size_y
    halo = REACH * size_y
    block = rows * lanes
    pack = LANES // cap
    lane8 = iota((8, LANES), 1)
    shift = lanes.bit_length() - 1

    def hot_rows(cell, move, index):
        return hot16(index, (cell >> shift) + move)

    def spread(cell, values):
        at = same16(zs, cell & (lanes - 1))
        stack = []
        for value in values:
            for part in parts_of(value, 2):
                stack.append(pick16(at, part))
        return jnp.concatenate(stack, axis=0)

    def inject(a, b):
        return lax.dot_general(
            jnp.concatenate(a, axis=1),
            jnp.concatenate(b, axis=1),
            NT_DIMS,
            preferred_element_type=jnp.float32,
        )

    zs = index16(LANES, LANES)
    row_index = index16(rows, LANES)
    halo_index = index16(halo, LANES)

    own_a, own_b, low_a, low_b, high_a, high_b = [], [], [], [], [], []
    mine, other = [], []
    for g in range(devices // pack):
        tiles = [got[g * pack + q] for q in range(pack)]
        one, two = tiles[0], tiles[pack // 2]
        for q in range(1, pack):
            later = lane8 >= q * cap
            one = jnp.where(later, tiles[q], one)
            two = jnp.where(later, tiles[(q + pack // 2) % pack], two)
        mine.append(one)
        other.append(two)
    for one in mine:
        cell = one[1:2].astype(jnp.int32)
        own_a.append(hot_rows(cell, 0, row_index))
        own_b.append(spread(cell, [one[0:1], one[2:3]]))
    for two in other:
        cell = two[1:2].astype(jnp.int32)
        low_a.append(hot_rows(cell, halo - rows, halo_index))
        low_b.append(spread(cell, [two[0:1]]))
    for two in other:
        cell = two[3:4].astype(jnp.int32)
        high_a.append(hot_rows(cell, 0, halo_index))
        high_b.append(spread(cell, [two[2:3]]))

    group = LANES // EDGE
    edge_parts = []
    for g in range(-(-devices // group)):
        total = got[g * group]
        for i in range(g * group + 1, min(devices, (g + 1) * group)):
            total = total + got[i]
        edge_parts.append(total)
    edge = jnp.concatenate(edge_parts, axis=1)
    width = edge.shape[1]
    spot = iota((8, width), 1)
    e = spot % EDGE
    count = edge[7:8]
    missing = jnp.zeros((8, width), jnp.float32)
    copies[0].wait()
    for reach in range(-SW, SW + 1):
        if reach == 0:
            continue
        if reach < 0:
            crosses = (e < -reach) & (spot >= -reach)
        else:
            crosses = (e >= EDGE - reach) & (spot < width - reach)
        keep = crosses & (count >= float(abs(reach)))
        missing = missing + jnp.where(
            keep, line_taps[reach + SW] * pltpu.roll(edge, (-reach) % width, 1), 0.0
        )
    edge_cell = edge[6:7].astype(jnp.int32) - me * block
    edge_row = jnp.clip(edge_cell >> shift, -2 * rows, 2 * rows)
    for g in range(width // LANES):
        at = slice(g * LANES, (g + 1) * LANES)
        b = spread(edge_cell[:, at], [missing[4:5, at], missing[5:6, at]])
        own_a.append(hot16(row_index, edge_row[:, at]))
        own_b.append(b)
        low_a.append(hot16(halo_index, edge_row[:, at] + halo))
        low_b.append(b[: 2 * LANES])
        high_a.append(hot16(halo_index, edge_row[:, at] - rows))
        high_b.append(b[: 2 * LANES])

    zeros = jnp.zeros((field.shape[0], PAD, lanes), jnp.float32)
    field[:, 0:PAD, :] = zeros
    field[:, PAD + size_y :, :] = zeros
    inside = slice(PAD, PAD + size_y)
    top = REACH + size_x

    out = inject(own_a, own_b)
    low_out = inject(low_a, low_b)
    high_out = inject(high_a, high_b)
    for copy in copies[1:]:
        copy.wait()
    first = (out[:, 0:lanes] + out[:, lanes : 2 * lanes]).reshape(size_x, size_y, lanes)
    source1[...] = (out[:, 2 * lanes : 3 * lanes] + out[:, 3 * lanes :]).reshape(
        size_x, size_y, lanes
    )
    field[REACH:top, inside, :] = free[REACH:top] + scale[REACH:top] * first
    done = [
        pltpu.make_async_copy(field.at[REACH:top, inside, :], prior_far, out_sems.at[0])
    ]
    done[0].start()
    first = (low_out[:, 0:lanes] + low_out[:, lanes:]).reshape(REACH, size_y, lanes)
    field[0:REACH, inside, :] = free[0:REACH] + scale[0:REACH] * first
    first = (high_out[:, 0:lanes] + high_out[:, lanes:]).reshape(REACH, size_y, lanes)
    field[top:, inside, :] = free[top:] + scale[top:] * first

    half = size_x // 2
    for part in range(2):
        planes = slice(part * half, (part + 1) * half)

        for x in range(part * half, (part + 1) * half):
            at = x + REACH
            fresh = field[at, inside, :]
            following = (
                2.0 * fresh
                - now[x]
                + scale[at] * (laplacian_plane(field, at, size_y) + source1[x])
            )
            last[x] = following
            gradient[x] = weight0[x] * fresh + weight1[x] * following

        done += started(
            out_sems.at[pl.ds(1 + 2 * part, 2)],
            (last.at[planes], last_far.at[planes]),
            (gradient.at[planes], gradient_far.at[planes]),
        )
    for copy in done:
        copy.wait()


def body(
    synthetic,
    observed,
    offsets,
    lines,
    owners,
    cells,
    taps,
    line_taps,
    velocity,
    adjoint_old,
    adjoint_now,
    forward,
):
    count = synthetic.shape[0]
    size_x, size_y, lanes = velocity.shape
    devices = lax.axis_size("sub")
    cap = max(2, 2 * count // devices)
    f32 = jnp.float32

    pair = [(i, i ^ 1) for i in range(devices)]
    following = [(i, i + 1) for i in range(1, devices - 1, 2)]
    following = following + [(b, a) for a, b in following]

    plane = (size_y, lanes)
    outer = size_x + 2 * REACH
    inner = pltpu.VMEM((size_x,) + plane, f32)
    padded = pltpu.VMEM((outer, size_y + 2 * PAD, lanes), f32)
    halo = pltpu.VMEM((3 * REACH,) + plane, f32)
    wider = pltpu.VMEM((outer,) + plane, f32)
    inner_far = pltpu.HBM((size_x,) + plane, f32)
    wider_far = pltpu.HBM((outer,) + plane, f32)
    dma = pltpu.SemaphoreType.DMA

    row = (1, count)
    small = pltpu.VMEM(row, jnp.int32)
    traces = pltpu.VMEM(synthetic.shape, f32)
    send, to_pair, to_next = pl.pallas_call(
        functools.partial(send_kernel, devices, cap, velocity.size),
        out_shape=(pltpu.HBM((devices, 8, LANES), f32), halo, halo),
        in_specs=[FAR] * 11,
        out_specs=(FAR, VMEM, VMEM),
        scratch_shapes=[
            small,
            small,
            pltpu.VMEM((1, taps.shape[0]), f32),
            small,
            pltpu.VMEM(lines.shape, jnp.int32),
            pltpu.VMEM((1, line_taps.shape[0]), f32),
            traces,
            traces,
            inner,
            inner,
            padded,
            pltpu.VMEM((devices, 8, LANES), f32),
            dma((12,)),
        ],
        compiler_params=PARAMS,
        name="send",
    )(
        *far(
            owners.reshape(row),
            cells.reshape(row),
            taps.reshape(1, -1),
            offsets.reshape(row),
            lines,
            line_taps.reshape(1, -1),
            synthetic,
            observed,
            adjoint_now,
            velocity,
            adjoint_old,
        )
    )
    from_next = lax.ppermute(to_next, "sub", following)
    from_pair = lax.ppermute(to_pair, "sub", pair)
    got = lax.all_to_all(send, "sub", split_axis=0, concat_axis=0, tiled=True)

    partial, now, vel, weight0, weight1 = pl.pallas_call(
        inner_kernel,
        out_shape=(inner,) * 3 + (inner_far,) * 2,
        in_specs=[FAR] * 4,
        out_specs=(VMEM,) * 5,
        scratch_shapes=[padded, inner, pltpu.VMEM(forward.shape, f32), dma((4,))],
        compiler_params=PARAMS,
        name="inner",
    )(*far(adjoint_old, adjoint_now, velocity, forward))
    free, scale = pl.pallas_call(
        first_kernel,
        out_shape=(wider,) * 2,
        in_specs=[VMEM] * 5,
        out_specs=(VMEM,) * 2,
        compiler_params=PARAMS,
        name="first",
    )(near(from_pair), near(from_next), near(partial), near(now), near(vel))

    field = jax.ShapeDtypeStruct((size_x,) + plane, f32)
    return pl.pallas_call(
        functools.partial(second_kernel, devices, cap),
        out_shape=(field, field, field),
        in_specs=[VMEM] * 3 + [FAR] * 4,
        out_specs=(FAR,) * 3,
        scratch_shapes=[
            pltpu.SMEM(line_taps.shape, f32),
            inner,
            inner,
            inner,
            inner,
            inner,
            pltpu.VMEM((outer, size_y + 2 * PAD, lanes), f32),
            inner,
            dma((4,)),
            dma((5,)),
        ],
        compiler_params=PARAMS,
        name="second",
    )(
        near(got),
        near(free),
        near(scale),
        *far(line_taps, adjoint_now, weight0, weight1),
    )


def solution(mesh):
    return jax.shard_map(
        body,
        mesh=mesh,
        in_specs=(
            P(("shot", "sub"), None),
            P(("shot", "sub"), None),
            P(("shot", "sub")),
            P(None, ("shot", "sub")),
            P(("shot", "sub"), None),
            P(("shot", "sub")),
            P(),
            P(),
            P("sub", None, None),
            P(("shot", "sub"), None, None),
            P(("shot", "sub"), None, None),
            P(None, ("shot", "sub"), None, None),
        ),
        out_specs=(
            P(("shot", "sub"), None, None),
            P(("shot", "sub"), None, None),
            P(("shot", "sub"), None, None),
        ),
        check_vma=False,
    )
```

time: 26.8 us -> 24.3 us (0.907)
  Pallas kernels: 14.6 us -> 9.58 us
  waiting for transfers between devices: 1.16 us -> 3.8 us
    pallas_call x4 -> x3, Pallas kernels: 9.94 us -> 6.23 us  [the longest x1 3.16 us: body(): pl.pallas_call(functools.partial(send_kernel, devices, cap, velocity.size...]
    all_to_all x1, waiting for transfers between devices: 1.15 us -> 3.79 us  [body(): got = lax.all_to_all(send, 'sub', split_axis=0, concat_axis=0, tiled=True)]
    pallas_call x1, Pallas kernels: 4.71 us -> 3.35 us  [body(): pl.pallas_call(functools.partial(second_kernel, devices, cap), out_shape=...]
  transfers between devices with their start and end apart: 3 -> 3, of which waited for: 1 -> 1; matrix products, arithmetic and copies ran while one was open for 0% -> 0% of each run, Pallas kernels for 29% -> 13%
where the time goes in v3:
time: 24.3 us; the launch traced here: 24 us
  starting transfers between devices  9.98 us (41%)
  Pallas kernels  9.58 us (39%)
  waiting for transfers between devices  3.8 us (16%)
  between operations  0.69 us (3%)
    all_to_all x1, starting transfers between devices, body(): got = lax.all_to_all(send, 'sub', split_axis=0, concat_axis=0, tiled=True)  8.79 us
    all_to_all x1, waiting for transfers between devices, body(): got = lax.all_to_all(send, 'sub', split_axis=0, concat_axis=0, tiled=True)  3.79 us
    pallas_call x1, Pallas kernels, body(): pl.pallas_call(functools.partial(second_kernel, devices, cap), out_shape=...  3.35 us
    pallas_call x1, Pallas kernels, body(): pl.pallas_call(functools.partial(send_kernel, devices, cap, velocity.size...  3.16 us
    pallas_call x1, Pallas kernels, body(): pl.pallas_call(inner_kernel, out_shape=(inner,) * 3 + (inner_far,) * 2, i...  2.9 us
    ppermute x1, starting transfers between devices, body(): from_next = lax.ppermute(to_next, 'sub', following)  0.67 us
    ppermute x1, starting transfers between devices, body(): from_pair = lax.ppermute(to_pair, 'sub', pair)  0.52 us
  transfers between devices with their start and end apart: 3, of which 1 were waited for; matrix products, arithmetic and copies ran while one was open for 0% of the time, Pallas kernels for 13%

profile of v3, /device:TPU:0, one launch (start us, length us, event | category | flops | bytes accessed | tf_op | source)
XLA Modules:
  0.0 24.0 jit_solution(12335758044322481785)
XLA Ops:
  0.6 3.2 %send.1 = (f32[16,8,128]{2,1,0:T(8,128)}, f32[12,64,128]{2,1,0:T(8,128)S(1)}, f32[12,64,128]{2,1,0:T(8,128)S(1)}) custom-call(s32[1,512]{1,0:T(1,128)} %bitcast.5, s32[1,512]{1,0:T(1,128)} %bitcast.6, f32[1,128]{1,0:T(1,128)} %bitcast.9, s32[1,512]{1,0:T(1,128)} %bitcast.7, s32[2,512]{1,0:T(2,128)} %lines_far.1, f32[1,9]{1,0:T(1,128)} %bitcast.8, ...), custom_call_target="tpu_custom_call" | custom-call | tf_op jit(solution)/shard_map/send/pallas_call | solution.py:577
  3.8 0.5 %collective-permute-start = (f32[12,64,128]{2,1,0:T(8,128)S(1)}, f32[12,64,128]{2,1,0:T(8,128)S(1)}, u32[]{:S(2)}, u32[]{:S(2)}) collective-permute-start(f32[12,64,128]{2,1,0:T(8,128)S(1)} %get-tuple-element.14), channel_id=1, source_target_pairs={{0,1},{1,0},{2,3},{3,2},{4,5},{5,4},{6,7},{7,6},{8,9},{9,8},{10,11... | collective-permute-start | bytes 1179656 | tf_op jit(solution)/shard_map/ppermute | solution.py:615
  4.3 0.7 %collective-permute-start.1 = (f32[12,64,128]{2,1,0:T(8,128)S(1)}, f32[12,64,128]{2,1,0:T(8,128)S(1)}, u32[]{:S(2)}, u32[]{:S(2)}) collective-permute-start(f32[12,64,128]{2,1,0:T(8,128)S(1)} %get-tuple-element.15), channel_id=1, source_target_pairs={{1,2},{3,4},{5,6},{7,8},{9,10},{11,12},{13,14},{2,1},{4,3},{6,5},{... | collective-permute-start | bytes 1179656 | tf_op jit(solution)/shard_map/ppermute | solution.py:614
  5.0 8.8 %all-to-all-start = ((f32[16,8,128]{2,1,0:T(8,128)}), f32[16,8,128]{2,1,0:T(8,128)S(1)}, u32[]{:S(2)}, u32[]{:S(2)}) async-start(f32[16,8,128]{2,1,0:T(8,128)} %get-tuple-element.13), calls=%async_computation | async-start | bytes 131072 | tf_op jit(solution)/shard_map/all_to_all | solution.py:616
  13.8 2.9 %inner.1 = (f32[8,64,128]{2,1,0:T(8,128)S(1)}, f32[8,64,128]{2,1,0:T(8,128)S(1)}, f32[8,64,128]{2,1,0:T(8,128)S(1)}, f32[8,64,128]{2,1,0:T(8,128)}, f32[8,64,128]{2,1,0:T(8,128)}) custom-call(f32[8,64,128]{2,1,0:T(8,128)} %old_far.3, f32[8,64,128]{2,1,0:T(8,128)} %now_far.5, f32[8,64,128]{2,1,0:T(8,128)} %vel_far.3, f32[4,8,64,128]{3,2,1,0:T(8,128)} %fwd_far.1), custom_call_target="tpu_custom_call" | custom-call | tf_op jit(solution)/shard_map/inner/pallas_call | solution.py:618
  16.7 0.0 collective-permute-done.from_pair
  16.7 0.0 collective-permute-done.1.from_next
  16.7 0.2 first.1
  16.9 3.8 %all-to-all-done.got = f32[16,8,128]{2,1,0:T(8,128)S(1)} async-done(((f32[16,8,128]{2,1,0:T(8,128)}), f32[16,8,128]{2,1,0:T(8,128)S(1)}, u32[]{:S(2)}, u32[]{:S(2)}) %all-to-all-start) | async-done | bytes 65568 | tf_op jit(solution)/shard_map/all_to_all | solution.py:616
  20.7 3.3 %second.1 = (f32[8,64,128]{2,1,0:T(8,128)}, f32[8,64,128]{2,1,0:T(8,128)}, f32[8,64,128]{2,1,0:T(8,128)}) custom-call(f32[16,8,128]{2,1,0:T(8,128)S(1)} %all-to-all-done.got, f32[16,64,128]{2,1,0:T(8,128)S(1)} %get-tuple-element.19.free, f32[16,64,128]{2,1,0:T(8,128)S(1)} %get-tuple-element.20.scale, f32[9]{0:T(128)} %line_taps_far.1, ...), custom_call_target="tpu_custom_call" | custom-call | tf_op jit(solution)/shard_map/second/pallas_call | solution.py:637
Async XLA Ops:
  3.8 12.9 %collective-permute-start = (f32[12,64,128]{2,1,0:T(8,128)S(1)}, f32[12,64,128]{2,1,0:T(8,128)S(1)}, u32[]{:S(2)}, u32[]{:S(2)}) collective-permute-start(f32[12,64,128]{2,1,0:T(8,128)S(1)} %get-tuple-element.14), channel_id=1, source_target_pairs={{0,1},{1,0},{2,3},{3,2},{4,5},{5,4},{6,7},{7,6},{8,9},{9,8},{10,11... | collective-permute-start | bytes 1179656 | tf_op jit(solution)/shard_map/ppermute | solution.py:615
  4.3 12.4 %collective-permute-start.1 = (f32[12,64,128]{2,1,0:T(8,128)S(1)}, f32[12,64,128]{2,1,0:T(8,128)S(1)}, u32[]{:S(2)}, u32[]{:S(2)}) collective-permute-start(f32[12,64,128]{2,1,0:T(8,128)S(1)} %get-tuple-element.15), channel_id=1, source_target_pairs={{1,2},{3,4},{5,6},{7,8},{9,10},{11,12},{13,14},{2,1},{4,3},{6,5},{... | collective-permute-start | bytes 1179656 | tf_op jit(solution)/shard_map/ppermute | solution.py:614
  5.0 15.7 %all-to-all-start = ((f32[16,8,128]{2,1,0:T(8,128)}), f32[16,8,128]{2,1,0:T(8,128)S(1)}, u32[]{:S(2)}, u32[]{:S(2)}) async-start(f32[16,8,128]{2,1,0:T(8,128)} %get-tuple-element.13), calls=%async_computation | async-start | bytes 131072 | tf_op jit(solution)/shard_map/all_to_all | solution.py:616

commit v4 on v3

--- a/solution.py
+++ b/solution.py
@@ -140,13 +140,13 @@
     copies = started(
         sems,
         (own_far, own),
+        (taps_far, taps),
+        (syn_far, syn),
+        (obs_far, obs),
         (cells_far, cells),
-        (taps_far, taps),
         (off_far, off),
         (lines_far, lines),
         (line_taps_far, line_taps),
-        (syn_far, syn),
-        (obs_far, obs),
         (now_far, wide.at[REACH : REACH + size_x, inside, :]),
         (vel_far, vel),
         (old_far, old),
@@ -157,7 +157,7 @@
     blank = jnp.zeros((REACH, size_y, lanes), jnp.float32)
     wide[0:REACH, inside, :] = blank
     wide[REACH + size_x :, inside, :] = blank
-    for copy in copies[:6]:
+    for copy in copies[:2]:
         copy.wait()
     me = lax.axis_index("sub")
     count, samples = syn.shape
@@ -194,18 +194,20 @@
     chosen = hot16(lane, edge_lane + (me % group) * EDGE)
 
     row = jnp.concatenate([taps[...], jnp.zeros((1, samples - ntap), jnp.float32)], axis=1)
-    starts = -(-(samples - ntap + 1) // 8) * 8
+    starts = -(-(samples - ntap + 1) // 16) * 16
     toeplitz = pltpu.roll(
         jnp.broadcast_to(row, (starts, samples)), 0, 1, stride=1, stride_axis=0
     )
-    for copy in copies[6:8]:
+    for copy in copies[2:-3]:
         copy.wait()
-    all_starts = lax.dot_general(
-        toeplitz,
-        syn[...] - obs[...],
-        NT_DIMS,
-        precision=lax.Precision.HIGHEST,
-        preferred_element_type=jnp.float32,
+    residual = syn[...] - obs[...]
+    r_high = residual.astype(jnp.bfloat16)
+    r_low = (residual - r_high.astype(jnp.float32)).astype(jnp.bfloat16)
+    t_high = toeplitz.astype(jnp.bfloat16)
+    t_low = (toeplitz - t_high.astype(jnp.float32)).astype(jnp.bfloat16)
+    all_starts = sum(
+        lax.dot_general(a, b, NT_DIMS, preferred_element_type=jnp.float32)
+        for a, b in ((t_high, r_low), (t_low, r_high), (t_high, r_high))
     )
     start = iota((starts, count), 0)
     offset = off[...]
@@ -266,9 +268,9 @@
     send[:, 5, :] = jnp.broadcast_to(edge[3:4] + edge[4:5] + edge[5:6], shape)
     send[:, 6, :] = jnp.broadcast_to(edge_cell, shape)
     send[:, 7, :] = jnp.broadcast_to(edge[9:10], shape)
-    sent = pltpu.make_async_copy(send, send_far, sems.at[11])
+    sent = pltpu.make_async_copy(send, send_far, sems.at[len(copies)])
     sent.start()
-    for copy in copies[8:]:
+    for copy in copies[-3:]:
         copy.wait()
     odd = me % 2
 
@@ -291,7 +293,23 @@
     sent.wait()
 
 
-def inner_kernel(old_far, now_far, vel_far, fwd_far, partial, now, vel, weight0, weight1, wide, old, fwd, sems):
+def inner_kernel(
+    old_far,
+    now_far,
+    vel_far,
+    fwd_far,
+    line_taps_far,
+    partial,
+    now,
+    vel,
+    weight0,
+    weight1,
+    line_taps,
+    wide,
+    old,
+    fwd,
+    sems,
+):
     size_x, size_y, lanes = old.shape
     inside = slice(PAD, PAD + size_y)
     copies = started(
@@ -300,6 +318,7 @@
         (vel_far, vel),
         (old_far, old),
         (fwd_far, fwd),
+        (line_taps_far, line_taps),
     )
     edge = jnp.zeros((wide.shape[0], PAD, lanes), jnp.float32)
     wide[:, 0:PAD, :] = edge
@@ -370,31 +389,19 @@
     got,
     free,
     scale,
-    line_taps_far,
-    now_far,
-    weight0_far,
-    weight1_far,
+    now,
+    weight0,
+    weight1,
+    line_taps,
     prior_far,
     last_far,
     gradient_far,
-    line_taps,
-    now,
-    weight0,
-    weight1,
     last,
     gradient,
     field,
     source1,
-    sems,
     out_sems,
 ):
-    copies = started(
-        sems,
-        (line_taps_far, line_taps),
-        (now_far, now),
-        (weight0_far, weight0),
-        (weight1_far, weight1),
-    )
     me = lax.axis_index("sub")
     size_x, size_y, lanes = now.shape
     rows = size_x * size_y
@@ -464,7 +471,6 @@
     e = spot % EDGE
     count = edge[7:8]
     missing = jnp.zeros((8, width), jnp.float32)
-    copies[0].wait()
     for reach in range(-SW, SW + 1):
         if reach == 0:
             continue
@@ -474,7 +480,9 @@
             crosses = (e >= EDGE - reach) & (spot < width - reach)
         keep = crosses & (count >= float(abs(reach)))
         missing = missing + jnp.where(
-            keep, line_taps[reach + SW] * pltpu.roll(edge, (-reach) % width, 1), 0.0
+            keep,
+            line_taps[0:1, reach + SW : reach + SW + 1] * pltpu.roll(edge, (-reach) % width, 1),
+            0.0,
         )
     edge_cell = edge[6:7].astype(jnp.int32) - me * block
     edge_row = jnp.clip(edge_cell >> shift, -2 * rows, 2 * rows)
@@ -497,8 +505,6 @@
     out = inject(own_a, own_b)
     low_out = inject(low_a, low_b)
     high_out = inject(high_a, high_b)
-    for copy in copies[1:]:
-        copy.wait()
     first = (out[:, 0:lanes] + out[:, lanes : 2 * lanes]).reshape(size_x, size_y, lanes)
     source1[...] = (out[:, 2 * lanes : 3 * lanes] + out[:, 3 * lanes :]).reshape(
         size_x, size_y, lanes
@@ -615,15 +621,15 @@
     from_pair = lax.ppermute(to_pair, "sub", pair)
     got = lax.all_to_all(send, "sub", split_axis=0, concat_axis=0, tiled=True)
 
-    partial, now, vel, weight0, weight1 = pl.pallas_call(
+    partial, now, vel, weight0, weight1, line_row = pl.pallas_call(
         inner_kernel,
-        out_shape=(inner,) * 3 + (inner_far,) * 2,
-        in_specs=[FAR] * 4,
-        out_specs=(VMEM,) * 5,
-        scratch_shapes=[padded, inner, pltpu.VMEM(forward.shape, f32), dma((4,))],
+        out_shape=(inner,) * 5 + (pltpu.VMEM((1, line_taps.shape[0]), f32),),
+        in_specs=[FAR] * 5,
+        out_specs=(VMEM,) * 6,
+        scratch_shapes=[padded, inner, pltpu.VMEM(forward.shape, f32), dma((5,))],
         compiler_params=PARAMS,
         name="inner",
-    )(*far(adjoint_old, adjoint_now, velocity, forward))
+    )(*far(adjoint_old, adjoint_now, velocity, forward, line_taps.reshape(1, -1)))
     free, scale = pl.pallas_call(
         first_kernel,
         out_shape=(wider,) * 2,
@@ -637,18 +643,13 @@
     return pl.pallas_call(
         functools.partial(second_kernel, devices, cap),
         out_shape=(field, field, field),
-        in_specs=[VMEM] * 3 + [FAR] * 4,
+        in_specs=[VMEM] * 7,
         out_specs=(FAR,) * 3,
         scratch_shapes=[
-            pltpu.SMEM(line_taps.shape, f32),
-            inner,
-            inner,
-            inner,
             inner,
             inner,
             pltpu.VMEM((outer, size_y + 2 * PAD, lanes), f32),
             inner,
-            dma((4,)),
             dma((5,)),
         ],
         compiler_params=PARAMS,
@@ -657,7 +658,10 @@
         near(got),
         near(free),
         near(scale),
-        *far(line_taps, adjoint_now, weight0, weight1),
+        near(now),
+        near(weight0),
+        near(weight1),
+        near(line_row),
     )
 
 

time: 24.3 us -> 23 us (0.947)
  Pallas kernels: 9.58 us -> 7.57 us
  waiting for transfers between devices: 3.8 us -> 4.53 us
    pallas_call x1, Pallas kernels: 3.35 us -> 2.37 us  [body(): pl.pallas_call(functools.partial(second_kernel, devices, cap), out_shape=...]
    pallas_call x1, Pallas kernels: 2.9 us -> 2.16 us  [body(): pl.pallas_call(inner_kernel, out_shape=(inner,) * 5 + (pltpu.VMEM((1, lin...]
    all_to_all x1, waiting for transfers between devices: 3.79 us -> 4.53 us  [body(): got = lax.all_to_all(send, 'sub', split_axis=0, concat_axis=0, tiled=True)]
    pallas_call x1, Pallas kernels: 3.16 us -> 2.87 us  [body(): pl.pallas_call(functools.partial(send_kernel, devices, cap, velocity.size...]
  transfers between devices with their start and end apart: 3 -> 3, of which waited for: 1 -> 1; matrix products, arithmetic and copies ran while one was open for 0% -> 0% of each run, Pallas kernels for 13% -> 10%
where the time goes in v4:
time: 23 us; the launch traced here: 22.8 us
  starting transfers between devices  9.98 us (43%)
  Pallas kernels  7.57 us (33%)
  waiting for transfers between devices  4.53 us (20%)
  between operations  0.69 us (3%)
    all_to_all x1, starting transfers between devices, body(): got = lax.all_to_all(send, 'sub', split_axis=0, concat_axis=0, tiled=True)  8.79 us
    all_to_all x1, waiting for transfers between devices, body(): got = lax.all_to_all(send, 'sub', split_axis=0, concat_axis=0, tiled=True)  4.53 us
    pallas_call x1, Pallas kernels, body(): pl.pallas_call(functools.partial(send_kernel, devices, cap, velocity.size...  2.87 us
    pallas_call x1, Pallas kernels, body(): pl.pallas_call(functools.partial(second_kernel, devices, cap), out_shape=...  2.37 us
    pallas_call x1, Pallas kernels, body(): pl.pallas_call(inner_kernel, out_shape=(inner,) * 5 + (pltpu.VMEM((1, lin...  2.16 us
    ppermute x1, starting transfers between devices, body(): from_next = lax.ppermute(to_next, 'sub', following)  0.67 us
    ppermute x1, starting transfers between devices, body(): from_pair = lax.ppermute(to_pair, 'sub', pair)  0.52 us
  transfers between devices with their start and end apart: 3, of which 1 were waited for; matrix products, arithmetic and copies ran while one was open for 0% of the time, Pallas kernels for 10%

profile of v4, /device:TPU:0, one launch (start us, length us, event | category | flops | bytes accessed | tf_op | source)
XLA Modules:
  0.0 22.8 jit_solution(6611961741676122203)
XLA Ops:
  0.6 2.9 %send.1 = (f32[16,8,128]{2,1,0:T(8,128)}, f32[12,64,128]{2,1,0:T(8,128)S(1)}, f32[12,64,128]{2,1,0:T(8,128)S(1)}) custom-call(s32[1,512]{1,0:T(1,128)} %bitcast.5, s32[1,512]{1,0:T(1,128)} %bitcast.6, f32[1,128]{1,0:T(1,128)} %bitcast.10, s32[1,512]{1,0:T(1,128)} %bitcast.7, s32[2,512]{1,0:T(2,128)} %lines_far.1, f32[1,9]{1,0:T(1,128)} %bitcast.8, ...), custom_call_target="tpu_custom_call" | custom-call | tf_op jit(solution)/shard_map/send/pallas_call | solution.py:583
  3.5 0.5 %collective-permute-start = (f32[12,64,128]{2,1,0:T(8,128)S(1)}, f32[12,64,128]{2,1,0:T(8,128)S(1)}, u32[]{:S(2)}, u32[]{:S(2)}) collective-permute-start(f32[12,64,128]{2,1,0:T(8,128)S(1)} %get-tuple-element.15), channel_id=1, source_target_pairs={{0,1},{1,0},{2,3},{3,2},{4,5},{5,4},{6,7},{7,6},{8,9},{9,8},{10,11... | collective-permute-start | bytes 1179656 | tf_op jit(solution)/shard_map/ppermute | solution.py:621
  4.0 0.7 %collective-permute-start.1 = (f32[12,64,128]{2,1,0:T(8,128)S(1)}, f32[12,64,128]{2,1,0:T(8,128)S(1)}, u32[]{:S(2)}, u32[]{:S(2)}) collective-permute-start(f32[12,64,128]{2,1,0:T(8,128)S(1)} %get-tuple-element.16), channel_id=1, source_target_pairs={{1,2},{3,4},{5,6},{7,8},{9,10},{11,12},{13,14},{2,1},{4,3},{6,5},{... | collective-permute-start | bytes 1179656 | tf_op jit(solution)/shard_map/ppermute | solution.py:620
  4.7 8.8 %all-to-all-start = ((f32[16,8,128]{2,1,0:T(8,128)}), f32[16,8,128]{2,1,0:T(8,128)S(1)}, u32[]{:S(2)}, u32[]{:S(2)}) async-start(f32[16,8,128]{2,1,0:T(8,128)} %get-tuple-element.14), calls=%async_computation | async-start | bytes 131072 | tf_op jit(solution)/shard_map/all_to_all | solution.py:622
  13.5 2.2 %inner.1 = (f32[8,64,128]{2,1,0:T(8,128)S(1)}, f32[8,64,128]{2,1,0:T(8,128)S(1)}, f32[8,64,128]{2,1,0:T(8,128)S(1)}, f32[8,64,128]{2,1,0:T(8,128)S(1)}, f32[8,64,128]{2,1,0:T(8,128)S(1)}, /*index=5*/f32[1,9]{1,0:T(1,128)S(1)}) custom-call(f32[8,64,128]{2,1,0:T(8,128)} %old_far.3, f32[8,64,128]{2,1,0:T(8,128)} %now_far.3, f32[8,64,128]{2,1,0:T(8,128)} %vel_far.3, ...), custom_call_target="tpu_custom_call" | custom-call | tf_op jit(solution)/shard_map/inner/pallas_call | solution.py:624
  15.7 0.0 collective-permute-done.from_pair
  15.7 0.0 collective-permute-done.1.from_next
  15.7 0.2 first.1
  15.9 4.5 %all-to-all-done.got = f32[16,8,128]{2,1,0:T(8,128)S(1)} async-done(((f32[16,8,128]{2,1,0:T(8,128)}), f32[16,8,128]{2,1,0:T(8,128)S(1)}, u32[]{:S(2)}, u32[]{:S(2)}) %all-to-all-start) | async-done | bytes 65568 | tf_op jit(solution)/shard_map/all_to_all | solution.py:622
  20.4 2.4 %second.1 = (f32[8,64,128]{2,1,0:T(8,128)}, f32[8,64,128]{2,1,0:T(8,128)}, f32[8,64,128]{2,1,0:T(8,128)}) custom-call(f32[16,8,128]{2,1,0:T(8,128)S(1)} %all-to-all-done.got, f32[16,64,128]{2,1,0:T(8,128)S(1)} %get-tuple-element.20.free, f32[16,64,128]{2,1,0:T(8,128)S(1)} %get-tuple-element.21.scale, f32[8,64,128]{2,1,0:T(8,128)S(1)} %get-tuple-element.18.now, ...), custom_call_target="tpu_custom_call" | custom-call | tf_op jit(solution)/shard_map/second/pallas_call | solution.py:643
Async XLA Ops:
  3.5 12.2 %collective-permute-start = (f32[12,64,128]{2,1,0:T(8,128)S(1)}, f32[12,64,128]{2,1,0:T(8,128)S(1)}, u32[]{:S(2)}, u32[]{:S(2)}) collective-permute-start(f32[12,64,128]{2,1,0:T(8,128)S(1)} %get-tuple-element.15), channel_id=1, source_target_pairs={{0,1},{1,0},{2,3},{3,2},{4,5},{5,4},{6,7},{7,6},{8,9},{9,8},{10,11... | collective-permute-start | bytes 1179656 | tf_op jit(solution)/shard_map/ppermute | solution.py:621
  4.0 11.7 %collective-permute-start.1 = (f32[12,64,128]{2,1,0:T(8,128)S(1)}, f32[12,64,128]{2,1,0:T(8,128)S(1)}, u32[]{:S(2)}, u32[]{:S(2)}) collective-permute-start(f32[12,64,128]{2,1,0:T(8,128)S(1)} %get-tuple-element.16), channel_id=1, source_target_pairs={{1,2},{3,4},{5,6},{7,8},{9,10},{11,12},{13,14},{2,1},{4,3},{6,5},{... | collective-permute-start | bytes 1179656 | tf_op jit(solution)/shard_map/ppermute | solution.py:620
  4.7 15.7 %all-to-all-start = ((f32[16,8,128]{2,1,0:T(8,128)}), f32[16,8,128]{2,1,0:T(8,128)S(1)}, u32[]{:S(2)}, u32[]{:S(2)}) async-start(f32[16,8,128]{2,1,0:T(8,128)} %get-tuple-element.14), calls=%async_computation | async-start | bytes 131072 | tf_op jit(solution)/shard_map/all_to_all | solution.py:622

commit v5 on v4

--- a/solution.py
+++ b/solution.py
@@ -105,6 +105,7 @@
 
 def send_kernel(
     devices,
+    place_of,
     cap,
     block,
     own_far,
@@ -248,10 +249,14 @@
     def to_lower(rows):
         return pltpu.roll(jnp.concatenate([rows[1:], none], axis=0), LANES // 2, 1)
 
-    send[:, 0, :] = value0 + to_upper(value0)
-    send[:, 1, :] = where + to_upper(where)
-    send[:, 2, :] = value1 + to_lower(value0)
-    send[:, 3, :] = to_lower(where)
+    def put(k, rows):
+        for to, at in enumerate(place_of):
+            send[at, k : k + 1, :] = rows[to : to + 1]
+
+    put(0, value0 + to_upper(value0))
+    put(1, where + to_upper(where))
+    put(2, value1 + to_lower(value0))
+    put(3, to_lower(where))
     count_ = jnp.where(place < SW, before, after).astype(jnp.float32)
     edge_rows = (
         parts_of(both[0:1], 3)
@@ -264,10 +269,10 @@
     edge = lax.dot_general(edge_rows, chosen, NT_DIMS, preferred_element_type=jnp.float32)
     edge_cell = edge[6:7] * float(block) + 256.0 * edge[7:8] + edge[8:9]
     shape = (devices, LANES)
-    send[:, 4, :] = jnp.broadcast_to(edge[0:1] + edge[1:2] + edge[2:3], shape)
-    send[:, 5, :] = jnp.broadcast_to(edge[3:4] + edge[4:5] + edge[5:6], shape)
-    send[:, 6, :] = jnp.broadcast_to(edge_cell, shape)
-    send[:, 7, :] = jnp.broadcast_to(edge[9:10], shape)
+    put(4, jnp.broadcast_to(edge[0:1] + edge[1:2] + edge[2:3], shape))
+    put(5, jnp.broadcast_to(edge[3:4] + edge[4:5] + edge[5:6], shape))
+    put(6, jnp.broadcast_to(edge_cell, shape))
+    put(7, jnp.broadcast_to(edge[9:10], shape))
     sent = pltpu.make_async_copy(send, send_far, sems.at[len(copies)])
     sent.start()
     for copy in copies[-3:]:
@@ -385,6 +390,7 @@
 
 def second_kernel(
     devices,
+    place_of,
     cap,
     got,
     free,
@@ -437,7 +443,7 @@
     own_a, own_b, low_a, low_b, high_a, high_b = [], [], [], [], [], []
     mine, other = [], []
     for g in range(devices // pack):
-        tiles = [got[g * pack + q] for q in range(pack)]
+        tiles = [got[place_of[g * pack + q]] for q in range(pack)]
         one, two = tiles[0], tiles[pack // 2]
         for q in range(1, pack):
             later = lane8 >= q * cap
@@ -461,9 +467,9 @@
     group = LANES // EDGE
     edge_parts = []
     for g in range(-(-devices // group)):
-        total = got[g * group]
+        total = got[place_of[g * group]]
         for i in range(g * group + 1, min(devices, (g + 1) * group)):
-            total = total + got[i]
+            total = total + got[place_of[i]]
         edge_parts.append(total)
     edge = jnp.concatenate(edge_parts, axis=1)
     width = edge.shape[1]
@@ -563,6 +569,8 @@
     cap = max(2, 2 * count // devices)
     f32 = jnp.float32
 
+    order = list(range(devices))[::-1]
+    place_of = [order.index(i) for i in range(devices)]
     pair = [(i, i ^ 1) for i in range(devices)]
     following = [(i, i + 1) for i in range(1, devices - 1, 2)]
     following = following + [(b, a) for a, b in following]
@@ -581,7 +589,7 @@
     small = pltpu.VMEM(row, jnp.int32)
     traces = pltpu.VMEM(synthetic.shape, f32)
     send, to_pair, to_next = pl.pallas_call(
-        functools.partial(send_kernel, devices, cap, velocity.size),
+        functools.partial(send_kernel, devices, place_of, cap, velocity.size),
         out_shape=(pltpu.HBM((devices, 8, LANES), f32), halo, halo),
         in_specs=[FAR] * 11,
         out_specs=(FAR, VMEM, VMEM),
@@ -619,7 +627,9 @@
     )
     from_next = lax.ppermute(to_next, "sub", following)
     from_pair = lax.ppermute(to_pair, "sub", pair)
-    got = lax.all_to_all(send, "sub", split_axis=0, concat_axis=0, tiled=True)
+    got = lax.all_to_all(
+        send, "sub", split_axis=0, concat_axis=0, axis_index_groups=[order], tiled=True
+    )
 
     partial, now, vel, weight0, weight1, line_row = pl.pallas_call(
         inner_kernel,
@@ -641,7 +651,7 @@
 
     field = jax.ShapeDtypeStruct((size_x,) + plane, f32)
     return pl.pallas_call(
-        functools.partial(second_kernel, devices, cap),
+        functools.partial(second_kernel, devices, place_of, cap),
         out_shape=(field, field, field),
         in_specs=[VMEM] * 7,
         out_specs=(FAR,) * 3,

time: 23 us -> 21.2 us (0.922)
  waiting for transfers between devices: 4.53 us -> 1.64 us
  starting transfers between devices: 9.98 us -> 11.1 us
    all_to_all x1, waiting for transfers between devices: 4.53 us -> 1.63 us  [body(): lax.all_to_all(send, 'sub', split_axis=0, concat_axis=0, axis_index_group...]
    all_to_all x1, starting transfers between devices: 8.79 us -> 9.86 us  [body(): lax.all_to_all(send, 'sub', split_axis=0, concat_axis=0, axis_index_group...]
  transfers between devices with their start and end apart: 3 -> 3, of which waited for: 1 -> 1; matrix products, arithmetic and copies ran while one was open for 0% -> 0% of each run, Pallas kernels for 10% -> 11%
where the time goes in v5:
time: 21.2 us; the launch traced here: 20.9 us
  starting transfers between devices  11.1 us (52%)
  Pallas kernels  7.57 us (36%)
  waiting for transfers between devices  1.64 us (8%)
  between operations  0.68 us (3%)
    all_to_all x1, starting transfers between devices, body(): lax.all_to_all(send, 'sub', split_axis=0, concat_axis=0, axis_index_group...  9.86 us
    pallas_call x1, Pallas kernels, body(): pl.pallas_call(functools.partial(send_kernel, devices, place_of, cap, vel...  2.86 us
    pallas_call x1, Pallas kernels, body(): pl.pallas_call(functools.partial(second_kernel, devices, place_of, cap),...  2.38 us
    pallas_call x1, Pallas kernels, body(): pl.pallas_call(inner_kernel, out_shape=(inner,) * 5 + (pltpu.VMEM((1, lin...  2.15 us
    all_to_all x1, waiting for transfers between devices, body(): lax.all_to_all(send, 'sub', split_axis=0, concat_axis=0, axis_index_group...  1.63 us
    ppermute x1, starting transfers between devices, body(): from_next = lax.ppermute(to_next, 'sub', following)  0.67 us
    ppermute x1, starting transfers between devices, body(): from_pair = lax.ppermute(to_pair, 'sub', pair)  0.52 us
  transfers between devices with their start and end apart: 3, of which 1 were waited for; matrix products, arithmetic and copies ran while one was open for 0% of the time, Pallas kernels for 11%

profile of v5, /device:TPU:0, one launch (start us, length us, event | category | flops | bytes accessed | tf_op | source)
XLA Modules:
  0.0 20.9 jit_solution(16697102107908390616)
XLA Ops:
  0.6 2.9 %send.1 = (f32[16,8,128]{2,1,0:T(8,128)}, f32[12,64,128]{2,1,0:T(8,128)S(1)}, f32[12,64,128]{2,1,0:T(8,128)S(1)}) custom-call(s32[1,512]{1,0:T(1,128)} %bitcast.5, s32[1,512]{1,0:T(1,128)} %bitcast.6, f32[1,128]{1,0:T(1,128)} %bitcast.10, s32[1,512]{1,0:T(1,128)} %bitcast.7, s32[2,512]{1,0:T(2,128)} %lines_far.1, f32[1,9]{1,0:T(1,128)} %bitcast.8, ...), custom_call_target="tpu_custom_call" | custom-call | tf_op jit(solution)/shard_map/send/pallas_call | solution.py:591
  3.5 0.5 %collective-permute-start = (f32[12,64,128]{2,1,0:T(8,128)S(1)}, f32[12,64,128]{2,1,0:T(8,128)S(1)}, u32[]{:S(2)}, u32[]{:S(2)}) collective-permute-start(f32[12,64,128]{2,1,0:T(8,128)S(1)} %get-tuple-element.15), channel_id=1, source_target_pairs={{0,1},{1,0},{2,3},{3,2},{4,5},{5,4},{6,7},{7,6},{8,9},{9,8},{10,11... | collective-permute-start | bytes 1179656 | tf_op jit(solution)/shard_map/ppermute | solution.py:629
  4.0 0.7 %collective-permute-start.1 = (f32[12,64,128]{2,1,0:T(8,128)S(1)}, f32[12,64,128]{2,1,0:T(8,128)S(1)}, u32[]{:S(2)}, u32[]{:S(2)}) collective-permute-start(f32[12,64,128]{2,1,0:T(8,128)S(1)} %get-tuple-element.16), channel_id=1, source_target_pairs={{1,2},{3,4},{5,6},{7,8},{9,10},{11,12},{13,14},{2,1},{4,3},{6,5},{... | collective-permute-start | bytes 1179656 | tf_op jit(solution)/shard_map/ppermute | solution.py:628
  4.7 9.9 %all-to-all-start = ((f32[16,8,128]{2,1,0:T(8,128)}), f32[16,8,128]{2,1,0:T(8,128)S(1)}, u32[]{:S(2)}, u32[]{:S(2)}) async-start(f32[16,8,128]{2,1,0:T(8,128)} %get-tuple-element.14), calls=%async_computation | async-start | bytes 131072 | tf_op jit(solution)/shard_map/all_to_all | solution.py:630
  14.6 2.2 %inner.1 = (f32[8,64,128]{2,1,0:T(8,128)S(1)}, f32[8,64,128]{2,1,0:T(8,128)S(1)}, f32[8,64,128]{2,1,0:T(8,128)S(1)}, f32[8,64,128]{2,1,0:T(8,128)S(1)}, f32[8,64,128]{2,1,0:T(8,128)S(1)}, /*index=5*/f32[1,9]{1,0:T(1,128)S(1)}) custom-call(f32[8,64,128]{2,1,0:T(8,128)} %old_far.3, f32[8,64,128]{2,1,0:T(8,128)} %now_far.3, f32[8,64,128]{2,1,0:T(8,128)} %vel_far.3, ...), custom_call_target="tpu_custom_call" | custom-call | tf_op jit(solution)/shard_map/inner/pallas_call | solution.py:634
  16.7 0.0 collective-permute-done.from_pair
  16.7 0.0 collective-permute-done.1.from_next
  16.7 0.2 first.1
  16.9 1.6 %all-to-all-done.got = f32[16,8,128]{2,1,0:T(8,128)S(1)} async-done(((f32[16,8,128]{2,1,0:T(8,128)}), f32[16,8,128]{2,1,0:T(8,128)S(1)}, u32[]{:S(2)}, u32[]{:S(2)}) %all-to-all-start) | async-done | bytes 65568 | tf_op jit(solution)/shard_map/all_to_all | solution.py:630
  18.6 2.4 %second.1 = (f32[8,64,128]{2,1,0:T(8,128)}, f32[8,64,128]{2,1,0:T(8,128)}, f32[8,64,128]{2,1,0:T(8,128)}) custom-call(f32[16,8,128]{2,1,0:T(8,128)S(1)} %all-to-all-done.got, f32[16,64,128]{2,1,0:T(8,128)S(1)} %get-tuple-element.20.free, f32[16,64,128]{2,1,0:T(8,128)S(1)} %get-tuple-element.21.scale, f32[8,64,128]{2,1,0:T(8,128)S(1)} %get-tuple-element.18.now, ...), custom_call_target="tpu_custom_call" | custom-call | tf_op jit(solution)/shard_map/second/pallas_call | solution.py:653
Async XLA Ops:
  3.5 13.2 %collective-permute-start = (f32[12,64,128]{2,1,0:T(8,128)S(1)}, f32[12,64,128]{2,1,0:T(8,128)S(1)}, u32[]{:S(2)}, u32[]{:S(2)}) collective-permute-start(f32[12,64,128]{2,1,0:T(8,128)S(1)} %get-tuple-element.15), channel_id=1, source_target_pairs={{0,1},{1,0},{2,3},{3,2},{4,5},{5,4},{6,7},{7,6},{8,9},{9,8},{10,11... | collective-permute-start | bytes 1179656 | tf_op jit(solution)/shard_map/ppermute | solution.py:629
  4.0 12.7 %collective-permute-start.1 = (f32[12,64,128]{2,1,0:T(8,128)S(1)}, f32[12,64,128]{2,1,0:T(8,128)S(1)}, u32[]{:S(2)}, u32[]{:S(2)}) collective-permute-start(f32[12,64,128]{2,1,0:T(8,128)S(1)} %get-tuple-element.16), channel_id=1, source_target_pairs={{1,2},{3,4},{5,6},{7,8},{9,10},{11,12},{13,14},{2,1},{4,3},{6,5},{... | collective-permute-start | bytes 1179656 | tf_op jit(solution)/shard_map/ppermute | solution.py:628
  4.7 13.9 %all-to-all-start = ((f32[16,8,128]{2,1,0:T(8,128)}), f32[16,8,128]{2,1,0:T(8,128)S(1)}, u32[]{:S(2)}, u32[]{:S(2)}) async-start(f32[16,8,128]{2,1,0:T(8,128)} %get-tuple-element.14), calls=%async_computation | async-start | bytes 131072 | tf_op jit(solution)/shard_map/all_to_all | solution.py:630

commit v6 on v5

--- a/solution.py
+++ b/solution.py
@@ -81,6 +81,17 @@
 
 
 PAD = 8
+
+
+class Planes:
+    def __init__(self, rows, height):
+        self.rows, self.height = rows, height
+
+    def __getitem__(self, i):
+        return self.rows[i * self.height : (i + 1) * self.height, :]
+
+    def __setitem__(self, i, value):
+        self.rows[i * self.height : (i + 1) * self.height, :] = value
 
 
 def laplacian_plane(field, x, size_y):
@@ -103,11 +114,26 @@
     return factor * factor
 
 
-def send_kernel(
-    devices,
-    place_of,
-    cap,
-    block,
+def half_block(target, start, wide, vel, old):
+    size_y = old.shape[1]
+    inside = slice(PAD, PAD + size_y)
+    for i in range(REACH):
+        x = start + i
+        own_now = wide[REACH + x, inside, :]
+        speed = vel[x]
+        target[i] = own_now
+        target[REACH + i] = (
+            2.0 * own_now
+            - old[x]
+            + squared(speed) * laplacian_plane(wide, x + REACH, size_y)
+        )
+        target[2 * REACH + i] = speed
+
+
+def next_kernel(
+    now_far,
+    vel_far,
+    old_far,
     own_far,
     cells_far,
     taps_far,
@@ -116,12 +142,10 @@
     line_taps_far,
     syn_far,
     obs_far,
-    now_far,
-    vel_far,
-    old_far,
-    send_far,
-    to_pair,
     to_next,
+    wide,
+    vel,
+    old,
     own,
     cells,
     taps,
@@ -130,27 +154,23 @@
     line_taps,
     syn,
     obs,
-    old,
-    vel,
-    wide,
-    send,
     sems,
 ):
     size_x, size_y, lanes = old.shape
     inside = slice(PAD, PAD + size_y)
     copies = started(
         sems,
+        (now_far, wide.at[REACH : REACH + size_x, inside, :]),
+        (vel_far, vel),
+        (old_far, old),
         (own_far, own),
+        (cells_far, cells),
         (taps_far, taps),
-        (syn_far, syn),
-        (obs_far, obs),
-        (cells_far, cells),
         (off_far, off),
         (lines_far, lines),
         (line_taps_far, line_taps),
-        (now_far, wide.at[REACH : REACH + size_x, inside, :]),
-        (vel_far, vel),
-        (old_far, old),
+        (syn_far, syn),
+        (obs_far, obs),
     )
     edge = jnp.zeros((wide.shape[0], PAD, lanes), jnp.float32)
     wide[:, 0:PAD, :] = edge
@@ -158,8 +178,37 @@
     blank = jnp.zeros((REACH, size_y, lanes), jnp.float32)
     wide[0:REACH, inside, :] = blank
     wide[REACH + size_x :, inside, :] = blank
-    for copy in copies[:2]:
+    for copy in copies[:3]:
         copy.wait()
+    odd = lax.axis_index("sub") % 2
+    used = 3 * REACH * size_y
+    to_next[used:, :] = jnp.zeros((to_next.shape[0] - used, lanes), jnp.float32)
+    half_block(Planes(to_next, size_y), (size_x - REACH) * odd, wide, vel, old)
+    for copy in copies[3:]:
+        copy.wait()
+
+
+def send_kernel(
+    devices,
+    place_of,
+    cap,
+    block,
+    wide,
+    vel,
+    old,
+    own,
+    cells,
+    taps,
+    off,
+    lines,
+    line_taps,
+    syn,
+    obs,
+    send_far,
+    to_pair,
+    send,
+    sems,
+):
     me = lax.axis_index("sub")
     count, samples = syn.shape
     ntap = taps.shape[1]
@@ -199,8 +248,6 @@
     toeplitz = pltpu.roll(
         jnp.broadcast_to(row, (starts, samples)), 0, 1, stride=1, stride_axis=0
     )
-    for copy in copies[2:-3]:
-        copy.wait()
     residual = syn[...] - obs[...]
     r_high = residual.astype(jnp.bfloat16)
     r_low = (residual - r_high.astype(jnp.float32)).astype(jnp.bfloat16)
@@ -273,28 +320,9 @@
     put(5, jnp.broadcast_to(edge[3:4] + edge[4:5] + edge[5:6], shape))
     put(6, jnp.broadcast_to(edge_cell, shape))
     put(7, jnp.broadcast_to(edge[9:10], shape))
-    sent = pltpu.make_async_copy(send, send_far, sems.at[len(copies)])
+    sent = pltpu.make_async_copy(send, send_far, sems.at[0])
     sent.start()
-    for copy in copies[-3:]:
-        copy.wait()
-    odd = me % 2
-
-    def half(target, start):
-        for i in range(REACH):
-            x = start + i
-            own_now = wide[REACH + x, inside, :]
-            speed = vel[x]
-            target[i] = own_now
-            target[REACH + i] = (
-                2.0 * own_now
-                - old[x]
-                + squared(speed) * laplacian_plane(wide, x + REACH, size_y)
-            )
-            target[2 * REACH + i] = speed
-
-    far_half = size_x - REACH
-    half(to_next, far_half * odd)
-    half(to_pair, far_half * (1 - odd))
+    half_block(to_pair, (old.shape[0] - REACH) * (1 - me % 2), wide, vel, old)
     sent.wait()
 
 
@@ -364,6 +392,7 @@
 ):
     odd = lax.axis_index("sub") % 2
     size_x = now.shape[0]
+    from_next = Planes(from_next, now.shape[1])
     top = REACH + size_x
 
     def border(source, first_out, low):
@@ -586,45 +615,38 @@
     dma = pltpu.SemaphoreType.DMA
 
     row = (1, count)
-    small = pltpu.VMEM(row, jnp.int32)
-    traces = pltpu.VMEM(synthetic.shape, f32)
-    send, to_pair, to_next = pl.pallas_call(
+    sources = (
+        adjoint_now,
+        velocity,
+        adjoint_old,
+        owners.reshape(row),
+        cells.reshape(row),
+        taps.reshape(1, -1),
+        offsets.reshape(row),
+        lines,
+        line_taps.reshape(1, -1),
+        synthetic,
+        observed,
+    )
+    fetched = (padded,) + tuple(pltpu.VMEM(a.shape, a.dtype) for a in sources[1:])
+    to_next, *fetched = pl.pallas_call(
+        next_kernel,
+        out_shape=(pltpu.VMEM((3 * REACH * size_y + 8, lanes), f32),) + fetched,
+        in_specs=[FAR] * len(sources),
+        out_specs=(VMEM,) * (1 + len(sources)),
+        scratch_shapes=[dma((len(sources),))],
+        compiler_params=PARAMS,
+        name="next",
+    )(*far(*sources))
+    send, to_pair = pl.pallas_call(
         functools.partial(send_kernel, devices, place_of, cap, velocity.size),
-        out_shape=(pltpu.HBM((devices, 8, LANES), f32), halo, halo),
-        in_specs=[FAR] * 11,
-        out_specs=(FAR, VMEM, VMEM),
-        scratch_shapes=[
-            small,
-            small,
-            pltpu.VMEM((1, taps.shape[0]), f32),
-            small,
-            pltpu.VMEM(lines.shape, jnp.int32),
-            pltpu.VMEM((1, line_taps.shape[0]), f32),
-            traces,
-            traces,
-            inner,
-            inner,
-            padded,
-            pltpu.VMEM((devices, 8, LANES), f32),
-            dma((12,)),
-        ],
+        out_shape=(pltpu.HBM((devices, 8, LANES), f32), halo),
+        in_specs=[VMEM] * len(fetched),
+        out_specs=(FAR, VMEM),
+        scratch_shapes=[pltpu.VMEM((devices, 8, LANES), f32), dma((1,))],
         compiler_params=PARAMS,
         name="send",
-    )(
-        *far(
-            owners.reshape(row),
-            cells.reshape(row),
-            taps.reshape(1, -1),
-            offsets.reshape(row),
-            lines,
-            line_taps.reshape(1, -1),
-            synthetic,
-            observed,
-            adjoint_now,
-            velocity,
-            adjoint_old,
-        )
-    )
+    )(*(near(a) for a in fetched))
     from_next = lax.ppermute(to_next, "sub", following)
     from_pair = lax.ppermute(to_pair, "sub", pair)
     got = lax.all_to_all(

time: 21.2 us -> 20.8 us (0.981)
  waiting for transfers between devices: 1.64 us -> 0.47 us
  starting transfers between devices: 11.1 us -> 11.5 us
  Pallas kernels: 7.57 us -> 7.86 us
    ppermute x1, starting transfers between devices: 0.52 us -> 4.37 us  [body(): from_pair = lax.ppermute(to_pair, 'sub', pair)]
    all_to_all x1, starting transfers between devices: 9.86 us -> 6.46 us  [body(): lax.all_to_all(send, 'sub', split_axis=0, concat_axis=0, axis_index_group...]
    pallas_call x0 -> x1, Pallas kernels: none -> 1.63 us  [body(): pl.pallas_call(next_kernel, out_shape=(pltpu.VMEM((3 * REACH * size_y + 8...]
    pallas_call x1, Pallas kernels: 2.86 us -> 1.53 us  [body(): pl.pallas_call(functools.partial(send_kernel, devices, place_of, cap, vel...]
    all_to_all x1, waiting for transfers between devices: 1.63 us -> 0.46 us  [body(): lax.all_to_all(send, 'sub', split_axis=0, concat_axis=0, axis_index_group...]
where the time goes in v6:
time: 20.8 us; the launch traced here: 20.5 us
  starting transfers between devices  11.5 us (55%)
  Pallas kernels  7.86 us (38%)
  between operations  0.69 us (3%)
  waiting for transfers between devices  0.47 us (2%)
    all_to_all x1, starting transfers between devices, body(): lax.all_to_all(send, 'sub', split_axis=0, concat_axis=0, axis_index_group...  6.46 us
    ppermute x1, starting transfers between devices, body(): from_pair = lax.ppermute(to_pair, 'sub', pair)  4.37 us
    pallas_call x1, Pallas kernels, body(): pl.pallas_call(functools.partial(second_kernel, devices, place_of, cap),...  2.37 us
    pallas_call x1, Pallas kernels, body(): pl.pallas_call(inner_kernel, out_shape=(inner,) * 5 + (pltpu.VMEM((1, lin...  2.15 us
    pallas_call x1, Pallas kernels, body(): pl.pallas_call(next_kernel, out_shape=(pltpu.VMEM((3 * REACH * size_y + 8...  1.63 us
    pallas_call x1, Pallas kernels, body(): pl.pallas_call(functools.partial(send_kernel, devices, place_of, cap, vel...  1.53 us
    ppermute x1, starting transfers between devices, body(): from_next = lax.ppermute(to_next, 'sub', following)  0.69 us
    all_to_all x1, waiting for transfers between devices, body(): lax.all_to_all(send, 'sub', split_axis=0, concat_axis=0, axis_index_group...  0.46 us
  transfers between devices with their start and end apart: 3, of which 1 were waited for; matrix products, arithmetic and copies ran while one was open for 0% of the time, Pallas kernels for 11%

profile of v6, /device:TPU:0, one launch (start us, length us, event | category | flops | bytes accessed | tf_op | source)
XLA Modules:
  0.0 20.5 jit_solution(16752649543796744016)
XLA Ops:
  0.6 1.6 %next.1 = (f32[776,128]{1,0:T(8,128)S(1)}, f32[16,80,128]{2,1,0:T(8,128)S(1)}, f32[8,64,128]{2,1,0:T(8,128)S(1)}, f32[8,64,128]{2,1,0:T(8,128)S(1)}, s32[1,512]{...) custom-call(f32[8,64,128]{2,1,0:T(8,128)} %now_far.3, ...), custom_call_target="tpu_custom_call" | custom-call | tf_op jit(solution)/shard_map/next/pallas_call | solution.py:632
  2.3 0.7 %collective-permute-start.1 = (f32[776,128]{1,0:T(8,128)S(1)}, f32[776,128]{1,0:T(8,128)S(1)}, u32[]{:S(2)}, u32[]{:S(2)}) collective-permute-start(f32[776,128]{1,0:T(8,128)S(1)} %get-tuple-element.38), channel_id=1, source_target_pairs={{1,2},{3,4},{5,6},{7,8},{9,10},{11,12},{13,14},{2,1},{4,3},{6,5},{... | collective-permute-start | bytes 1191944 | tf_op jit(solution)/shard_map/ppermute | solution.py:650
  3.0 1.5 %send.1 = (f32[16,8,128]{2,1,0:T(8,128)}, f32[12,64,128]{2,1,0:T(8,128)S(1)}) custom-call(f32[16,80,128]{2,1,0:T(8,128)S(1)} %get-tuple-element.25.wide, f32[8,64,128]{2,1,0:T(8,128)S(1)} %get-tuple-element.26.vel, f32[8,64,128]{2,1,0:T(8,128)S(1)} %get-tuple-element.27.old, s32[1,512]{1,0:T(1,128)S(1)} %get-tuple-element.28.own, ...), custom_call_target="tpu_custom_call" | custom-call | tf_op jit(solution)/shard_map/send/pallas_call | solution.py:641
  4.5 4.4 %collective-permute-start = (f32[12,64,128]{2,1,0:T(8,128)S(1)}, f32[12,64,128]{2,1,0:T(8,128)S(1)}, u32[]{:S(2)}, u32[]{:S(2)}) collective-permute-start(f32[12,64,128]{2,1,0:T(8,128)S(1)} %get-tuple-element.37), channel_id=1, source_target_pairs={{0,1},{1,0},{2,3},{3,2},{4,5},{5,4},{6,7},{7,6},{8,9},{9,8},{10,11... | collective-permute-start | bytes 1179656 | tf_op jit(solution)/shard_map/ppermute | solution.py:651
  8.9 6.5 %all-to-all-start = ((f32[16,8,128]{2,1,0:T(8,128)}), f32[16,8,128]{2,1,0:T(8,128)S(1)}, u32[]{:S(2)}, u32[]{:S(2)}) async-start(f32[16,8,128]{2,1,0:T(8,128)} %get-tuple-element.36), calls=%async_computation | async-start | bytes 131072 | tf_op jit(solution)/shard_map/all_to_all | solution.py:652
  15.3 2.2 %inner.1 = (f32[8,64,128]{2,1,0:T(8,128)S(1)}, f32[8,64,128]{2,1,0:T(8,128)S(1)}, f32[8,64,128]{2,1,0:T(8,128)S(1)}, f32[8,64,128]{2,1,0:T(8,128)S(1)}, f32[8,64,128]{2,1,0:T(8,128)S(1)}, /*index=5*/f32[1,9]{1,0:T(1,128)S(1)}) custom-call(f32[8,64,128]{2,1,0:T(8,128)} %old_far.3, f32[8,64,128]{2,1,0:T(8,128)} %now_far.3, f32[8,64,128]{2,1,0:T(8,128)} %vel_far.3, ...), custom_call_target="tpu_custom_call" | custom-call | tf_op jit(solution)/shard_map/inner/pallas_call | solution.py:656
  17.5 0.0 collective-permute-done.from_pair
  17.5 0.0 collective-permute-done.1.from_next
  17.5 0.2 first.1
  17.7 0.5 %all-to-all-done.got = f32[16,8,128]{2,1,0:T(8,128)S(1)} async-done(((f32[16,8,128]{2,1,0:T(8,128)}), f32[16,8,128]{2,1,0:T(8,128)S(1)}, u32[]{:S(2)}, u32[]{:S(2)}) %all-to-all-start) | async-done | bytes 65568 | tf_op jit(solution)/shard_map/all_to_all | solution.py:652
  18.2 2.4 %second.1 = (f32[8,64,128]{2,1,0:T(8,128)}, f32[8,64,128]{2,1,0:T(8,128)}, f32[8,64,128]{2,1,0:T(8,128)}) custom-call(f32[16,8,128]{2,1,0:T(8,128)S(1)} %all-to-all-done.got, f32[16,64,128]{2,1,0:T(8,128)S(1)} %get-tuple-element.42.free, f32[16,64,128]{2,1,0:T(8,128)S(1)} %get-tuple-element.43.scale, f32[8,64,128]{2,1,0:T(8,128)S(1)} %get-tuple-element.40.now, ...), custom_call_target="tpu_custom_call" | custom-call | tf_op jit(solution)/shard_map/second/pallas_call | solution.py:675
Async XLA Ops:
  2.3 15.2 %collective-permute-start.1 = (f32[776,128]{1,0:T(8,128)S(1)}, f32[776,128]{1,0:T(8,128)S(1)}, u32[]{:S(2)}, u32[]{:S(2)}) collective-permute-start(f32[776,128]{1,0:T(8,128)S(1)} %get-tuple-element.38), channel_id=1, source_target_pairs={{1,2},{3,4},{5,6},{7,8},{9,10},{11,12},{13,14},{2,1},{4,3},{6,5},{... | collective-permute-start | bytes 1191944 | tf_op jit(solution)/shard_map/ppermute | solution.py:650
  4.5 13.0 %collective-permute-start = (f32[12,64,128]{2,1,0:T(8,128)S(1)}, f32[12,64,128]{2,1,0:T(8,128)S(1)}, u32[]{:S(2)}, u32[]{:S(2)}) collective-permute-start(f32[12,64,128]{2,1,0:T(8,128)S(1)} %get-tuple-element.37), channel_id=1, source_target_pairs={{0,1},{1,0},{2,3},{3,2},{4,5},{5,4},{6,7},{7,6},{8,9},{9,8},{10,11... | collective-permute-start | bytes 1179656 | tf_op jit(solution)/shard_map/ppermute | solution.py:651
  8.9 9.3 %all-to-all-start = ((f32[16,8,128]{2,1,0:T(8,128)}), f32[16,8,128]{2,1,0:T(8,128)S(1)}, u32[]{:S(2)}, u32[]{:S(2)}) async-start(f32[16,8,128]{2,1,0:T(8,128)} %get-tuple-element.36), calls=%async_computation | async-start | bytes 131072 | tf_op jit(solution)/shard_map/all_to_all | solution.py:652

commit v7 on v6

--- a/solution.py
+++ b/solution.py
@@ -554,11 +554,11 @@
     first = (high_out[:, 0:lanes] + high_out[:, lanes:]).reshape(REACH, size_y, lanes)
     field[top:, inside, :] = free[top:] + scale[top:] * first
 
-    half = size_x // 2
-    for part in range(2):
-        planes = slice(part * half, (part + 1) * half)
-
-        for x in range(part * half, (part + 1) * half):
+    cuts = (0, size_x // 2, size_x - 1, size_x)
+    for part in range(3):
+        planes = slice(cuts[part], cuts[part + 1])
+
+        for x in range(cuts[part], cuts[part + 1]):
             at = x + REACH
             fresh = field[at, inside, :]
             following = (
@@ -598,7 +598,7 @@
     cap = max(2, 2 * count // devices)
     f32 = jnp.float32
 
-    order = list(range(devices))[::-1]
+    order = list(range(1, devices, 2))[::-1] + list(range(0, devices, 2))[::-1]
     place_of = [order.index(i) for i in range(devices)]
     pair = [(i, i ^ 1) for i in range(devices)]
     following = [(i, i + 1) for i in range(1, devices - 1, 2)]
@@ -682,7 +682,7 @@
             inner,
             pltpu.VMEM((outer, size_y + 2 * PAD, lanes), f32),
             inner,
-            dma((5,)),
+            dma((7,)),
         ],
         compiler_params=PARAMS,
         name="second",

time: 20.8 us -> 20.7 us (level)
  no operation moved by 1% of the time
where the time goes in v7:
time: 20.7 us; the launch traced here: 20.4 us
  starting transfers between devices  11.5 us (56%)
  Pallas kernels  7.84 us (38%)
  between operations  0.69 us (3%)
  waiting for transfers between devices  0.42 us (2%)
    all_to_all x1, starting transfers between devices, body(): lax.all_to_all(send, 'sub', split_axis=0, concat_axis=0, axis_index_group...  6.43 us
    ppermute x1, starting transfers between devices, body(): from_pair = lax.ppermute(to_pair, 'sub', pair)  4.37 us
    pallas_call x1, Pallas kernels, body(): pl.pallas_call(functools.partial(second_kernel, devices, place_of, cap),...  2.35 us
    pallas_call x1, Pallas kernels, body(): pl.pallas_call(inner_kernel, out_shape=(inner,) * 5 + (pltpu.VMEM((1, lin...  2.15 us
    pallas_call x1, Pallas kernels, body(): pl.pallas_call(next_kernel, out_shape=(pltpu.VMEM((3 * REACH * size_y + 8...  1.63 us
    pallas_call x1, Pallas kernels, body(): pl.pallas_call(functools.partial(send_kernel, devices, place_of, cap, vel...  1.53 us
    ppermute x1, starting transfers between devices, body(): from_next = lax.ppermute(to_next, 'sub', following)  0.69 us
  transfers between devices with their start and end apart: 3, of which 1 were waited for; matrix products, arithmetic and copies ran while one was open for 0% of the time, Pallas kernels for 11%

profile of v7, /device:TPU:0, one launch (start us, length us, event | category | flops | bytes accessed | tf_op | source)
XLA Modules:
  0.0 20.4 jit_solution(17243220911903685226)
XLA Ops:
  0.6 1.6 %next.1 = (f32[776,128]{1,0:T(8,128)S(1)}, f32[16,80,128]{2,1,0:T(8,128)S(1)}, f32[8,64,128]{2,1,0:T(8,128)S(1)}, f32[8,64,128]{2,1,0:T(8,128)S(1)}, s32[1,512]{...) custom-call(f32[8,64,128]{2,1,0:T(8,128)} %now_far.3, ...), custom_call_target="tpu_custom_call" | custom-call | tf_op jit(solution)/shard_map/next/pallas_call | solution.py:632
  2.3 0.7 %collective-permute-start.1 = (f32[776,128]{1,0:T(8,128)S(1)}, f32[776,128]{1,0:T(8,128)S(1)}, u32[]{:S(2)}, u32[]{:S(2)}) collective-permute-start(f32[776,128]{1,0:T(8,128)S(1)} %get-tuple-element.38), channel_id=1, source_target_pairs={{1,2},{3,4},{5,6},{7,8},{9,10},{11,12},{13,14},{2,1},{4,3},{6,5},{... | collective-permute-start | bytes 1191944 | tf_op jit(solution)/shard_map/ppermute | solution.py:650
  3.0 1.5 %send.1 = (f32[16,8,128]{2,1,0:T(8,128)}, f32[12,64,128]{2,1,0:T(8,128)S(1)}) custom-call(f32[16,80,128]{2,1,0:T(8,128)S(1)} %get-tuple-element.25.wide, f32[8,64,128]{2,1,0:T(8,128)S(1)} %get-tuple-element.26.vel, f32[8,64,128]{2,1,0:T(8,128)S(1)} %get-tuple-element.27.old, s32[1,512]{1,0:T(1,128)S(1)} %get-tuple-element.28.own, ...), custom_call_target="tpu_custom_call" | custom-call | tf_op jit(solution)/shard_map/send/pallas_call | solution.py:641
  4.5 4.4 %collective-permute-start = (f32[12,64,128]{2,1,0:T(8,128)S(1)}, f32[12,64,128]{2,1,0:T(8,128)S(1)}, u32[]{:S(2)}, u32[]{:S(2)}) collective-permute-start(f32[12,64,128]{2,1,0:T(8,128)S(1)} %get-tuple-element.37), channel_id=1, source_target_pairs={{0,1},{1,0},{2,3},{3,2},{4,5},{5,4},{6,7},{7,6},{8,9},{9,8},{10,11... | collective-permute-start | bytes 1179656 | tf_op jit(solution)/shard_map/ppermute | solution.py:651
  8.9 6.4 %all-to-all-start = ((f32[16,8,128]{2,1,0:T(8,128)}), f32[16,8,128]{2,1,0:T(8,128)S(1)}, u32[]{:S(2)}, u32[]{:S(2)}) async-start(f32[16,8,128]{2,1,0:T(8,128)} %get-tuple-element.36), calls=%async_computation | async-start | bytes 131072 | tf_op jit(solution)/shard_map/all_to_all | solution.py:652
  15.3 2.2 %inner.1 = (f32[8,64,128]{2,1,0:T(8,128)S(1)}, f32[8,64,128]{2,1,0:T(8,128)S(1)}, f32[8,64,128]{2,1,0:T(8,128)S(1)}, f32[8,64,128]{2,1,0:T(8,128)S(1)}, f32[8,64,128]{2,1,0:T(8,128)S(1)}, /*index=5*/f32[1,9]{1,0:T(1,128)S(1)}) custom-call(f32[8,64,128]{2,1,0:T(8,128)} %old_far.3, f32[8,64,128]{2,1,0:T(8,128)} %now_far.3, f32[8,64,128]{2,1,0:T(8,128)} %vel_far.3, ...), custom_call_target="tpu_custom_call" | custom-call | tf_op jit(solution)/shard_map/inner/pallas_call | solution.py:656
  17.5 0.0 collective-permute-done.from_pair
  17.5 0.0 collective-permute-done.1.from_next
  17.5 0.2 first.1
  17.7 0.4 %all-to-all-done.got = f32[16,8,128]{2,1,0:T(8,128)S(1)} async-done(((f32[16,8,128]{2,1,0:T(8,128)}), f32[16,8,128]{2,1,0:T(8,128)S(1)}, u32[]{:S(2)}, u32[]{:S(2)}) %all-to-all-start) | async-done | bytes 65568 | tf_op jit(solution)/shard_map/all_to_all | solution.py:652
  18.1 2.4 %second.1 = (f32[8,64,128]{2,1,0:T(8,128)}, f32[8,64,128]{2,1,0:T(8,128)}, f32[8,64,128]{2,1,0:T(8,128)}) custom-call(f32[16,8,128]{2,1,0:T(8,128)S(1)} %all-to-all-done.got, f32[16,64,128]{2,1,0:T(8,128)S(1)} %get-tuple-element.42.free, f32[16,64,128]{2,1,0:T(8,128)S(1)} %get-tuple-element.43.scale, f32[8,64,128]{2,1,0:T(8,128)S(1)} %get-tuple-element.40.now, ...), custom_call_target="tpu_custom_call" | custom-call | tf_op jit(solution)/shard_map/second/pallas_call | solution.py:675
Async XLA Ops:
  2.3 15.2 %collective-permute-start.1 = (f32[776,128]{1,0:T(8,128)S(1)}, f32[776,128]{1,0:T(8,128)S(1)}, u32[]{:S(2)}, u32[]{:S(2)}) collective-permute-start(f32[776,128]{1,0:T(8,128)S(1)} %get-tuple-element.38), channel_id=1, source_target_pairs={{1,2},{3,4},{5,6},{7,8},{9,10},{11,12},{13,14},{2,1},{4,3},{6,5},{... | collective-permute-start | bytes 1191944 | tf_op jit(solution)/shard_map/ppermute | solution.py:650
  4.5 13.0 %collective-permute-start = (f32[12,64,128]{2,1,0:T(8,128)S(1)}, f32[12,64,128]{2,1,0:T(8,128)S(1)}, u32[]{:S(2)}, u32[]{:S(2)}) collective-permute-start(f32[12,64,128]{2,1,0:T(8,128)S(1)} %get-tuple-element.37), channel_id=1, source_target_pairs={{0,1},{1,0},{2,3},{3,2},{4,5},{5,4},{6,7},{7,6},{8,9},{9,8},{10,11... | collective-permute-start | bytes 1179656 | tf_op jit(solution)/shard_map/ppermute | solution.py:651
  8.9 9.2 %all-to-all-start = ((f32[16,8,128]{2,1,0:T(8,128)}), f32[16,8,128]{2,1,0:T(8,128)S(1)}, u32[]{:S(2)}, u32[]{:S(2)}) async-start(f32[16,8,128]{2,1,0:T(8,128)} %get-tuple-element.36), calls=%async_computation | async-start | bytes 131072 | tf_op jit(solution)/shard_map/all_to_all | solution.py:652

commit v8 on v6

--- a/solution.py
+++ b/solution.py
@@ -156,6 +156,8 @@
     obs,
     sems,
 ):
+    piece = syn.shape[0] // 2
+    cuts = [pl.ds(i * piece, piece) for i in range(2)]
     size_x, size_y, lanes = old.shape
     inside = slice(PAD, PAD + size_y)
     copies = started(
@@ -163,14 +165,14 @@
         (now_far, wide.at[REACH : REACH + size_x, inside, :]),
         (vel_far, vel),
         (old_far, old),
+        *((syn_far.at[cut], syn.at[cut]) for cut in cuts),
+        *((obs_far.at[cut], obs.at[cut]) for cut in cuts),
         (own_far, own),
         (cells_far, cells),
         (taps_far, taps),
         (off_far, off),
         (lines_far, lines),
         (line_taps_far, line_taps),
-        (syn_far, syn),
-        (obs_far, obs),
     )
     edge = jnp.zeros((wide.shape[0], PAD, lanes), jnp.float32)
     wide[:, 0:PAD, :] = edge
@@ -634,7 +636,7 @@
         out_shape=(pltpu.VMEM((3 * REACH * size_y + 8, lanes), f32),) + fetched,
         in_specs=[FAR] * len(sources),
         out_specs=(VMEM,) * (1 + len(sources)),
-        scratch_shapes=[dma((len(sources),))],
+        scratch_shapes=[dma((len(sources) + 2,))],
         compiler_params=PARAMS,
         name="next",
     )(*far(*sources))

time: 20.8 us -> 20.8 us (level)
  no operation moved by 1% of the time
where the time goes in v8:
time: 20.8 us; the launch traced here: 20.5 us
  starting transfers between devices  11.5 us (55%)
  Pallas kernels  7.85 us (38%)
  between operations  0.69 us (3%)
  waiting for transfers between devices  0.47 us (2%)
    all_to_all x1, starting transfers between devices, body(): lax.all_to_all(send, 'sub', split_axis=0, concat_axis=0, axis_index_group...  6.46 us
    ppermute x1, starting transfers between devices, body(): from_pair = lax.ppermute(to_pair, 'sub', pair)  4.37 us
    pallas_call x1, Pallas kernels, body(): pl.pallas_call(functools.partial(second_kernel, devices, place_of, cap),...  2.37 us
    pallas_call x1, Pallas kernels, body(): pl.pallas_call(inner_kernel, out_shape=(inner,) * 5 + (pltpu.VMEM((1, lin...  2.15 us
    pallas_call x1, Pallas kernels, body(): pl.pallas_call(next_kernel, out_shape=(pltpu.VMEM((3 * REACH * size_y + 8...  1.63 us
    pallas_call x1, Pallas kernels, body(): pl.pallas_call(functools.partial(send_kernel, devices, place_of, cap, vel...  1.53 us
    ppermute x1, starting transfers between devices, body(): from_next = lax.ppermute(to_next, 'sub', following)  0.69 us
    all_to_all x1, waiting for transfers between devices, body(): lax.all_to_all(send, 'sub', split_axis=0, concat_axis=0, axis_index_group...  0.46 us
  transfers between devices with their start and end apart: 3, of which 1 were waited for; matrix products, arithmetic and copies ran while one was open for 0% of the time, Pallas kernels for 11%

profile of v8, /device:TPU:0, one launch (start us, length us, event | category | flops | bytes accessed | tf_op | source)
XLA Modules:
  0.0 20.5 jit_solution(5720936135626283900)
XLA Ops:
  0.6 1.6 %next.1 = (f32[776,128]{1,0:T(8,128)S(1)}, f32[16,80,128]{2,1,0:T(8,128)S(1)}, f32[8,64,128]{2,1,0:T(8,128)S(1)}, f32[8,64,128]{2,1,0:T(8,128)S(1)}, s32[1,512]{...) custom-call(f32[8,64,128]{2,1,0:T(8,128)} %now_far.3, ...), custom_call_target="tpu_custom_call" | custom-call | tf_op jit(solution)/shard_map/next/pallas_call | solution.py:634
  2.3 0.7 %collective-permute-start.1 = (f32[776,128]{1,0:T(8,128)S(1)}, f32[776,128]{1,0:T(8,128)S(1)}, u32[]{:S(2)}, u32[]{:S(2)}) collective-permute-start(f32[776,128]{1,0:T(8,128)S(1)} %get-tuple-element.38), channel_id=1, source_target_pairs={{1,2},{3,4},{5,6},{7,8},{9,10},{11,12},{13,14},{2,1},{4,3},{6,5},{... | collective-permute-start | bytes 1191944 | tf_op jit(solution)/shard_map/ppermute | solution.py:652
  3.0 1.5 %send.1 = (f32[16,8,128]{2,1,0:T(8,128)}, f32[12,64,128]{2,1,0:T(8,128)S(1)}) custom-call(f32[16,80,128]{2,1,0:T(8,128)S(1)} %get-tuple-element.25.wide, f32[8,64,128]{2,1,0:T(8,128)S(1)} %get-tuple-element.26.vel, f32[8,64,128]{2,1,0:T(8,128)S(1)} %get-tuple-element.27.old, s32[1,512]{1,0:T(1,128)S(1)} %get-tuple-element.28.own, ...), custom_call_target="tpu_custom_call" | custom-call | tf_op jit(solution)/shard_map/send/pallas_call | solution.py:643
  4.5 4.4 %collective-permute-start = (f32[12,64,128]{2,1,0:T(8,128)S(1)}, f32[12,64,128]{2,1,0:T(8,128)S(1)}, u32[]{:S(2)}, u32[]{:S(2)}) collective-permute-start(f32[12,64,128]{2,1,0:T(8,128)S(1)} %get-tuple-element.37), channel_id=1, source_target_pairs={{0,1},{1,0},{2,3},{3,2},{4,5},{5,4},{6,7},{7,6},{8,9},{9,8},{10,11... | collective-permute-start | bytes 1179656 | tf_op jit(solution)/shard_map/ppermute | solution.py:653
  8.9 6.5 %all-to-all-start = ((f32[16,8,128]{2,1,0:T(8,128)}), f32[16,8,128]{2,1,0:T(8,128)S(1)}, u32[]{:S(2)}, u32[]{:S(2)}) async-start(f32[16,8,128]{2,1,0:T(8,128)} %get-tuple-element.36), calls=%async_computation | async-start | bytes 131072 | tf_op jit(solution)/shard_map/all_to_all | solution.py:654
  15.3 2.2 %inner.1 = (f32[8,64,128]{2,1,0:T(8,128)S(1)}, f32[8,64,128]{2,1,0:T(8,128)S(1)}, f32[8,64,128]{2,1,0:T(8,128)S(1)}, f32[8,64,128]{2,1,0:T(8,128)S(1)}, f32[8,64,128]{2,1,0:T(8,128)S(1)}, /*index=5*/f32[1,9]{1,0:T(1,128)S(1)}) custom-call(f32[8,64,128]{2,1,0:T(8,128)} %old_far.3, f32[8,64,128]{2,1,0:T(8,128)} %now_far.3, f32[8,64,128]{2,1,0:T(8,128)} %vel_far.3, ...), custom_call_target="tpu_custom_call" | custom-call | tf_op jit(solution)/shard_map/inner/pallas_call | solution.py:658
  17.5 0.0 collective-permute-done.from_pair
  17.5 0.0 collective-permute-done.1.from_next
  17.5 0.2 first.1
  17.7 0.5 %all-to-all-done.got = f32[16,8,128]{2,1,0:T(8,128)S(1)} async-done(((f32[16,8,128]{2,1,0:T(8,128)}), f32[16,8,128]{2,1,0:T(8,128)S(1)}, u32[]{:S(2)}, u32[]{:S(2)}) %all-to-all-start) | async-done | bytes 65568 | tf_op jit(solution)/shard_map/all_to_all | solution.py:654
  18.2 2.4 %second.1 = (f32[8,64,128]{2,1,0:T(8,128)}, f32[8,64,128]{2,1,0:T(8,128)}, f32[8,64,128]{2,1,0:T(8,128)}) custom-call(f32[16,8,128]{2,1,0:T(8,128)S(1)} %all-to-all-done.got, f32[16,64,128]{2,1,0:T(8,128)S(1)} %get-tuple-element.42.free, f32[16,64,128]{2,1,0:T(8,128)S(1)} %get-tuple-element.43.scale, f32[8,64,128]{2,1,0:T(8,128)S(1)} %get-tuple-element.40.now, ...), custom_call_target="tpu_custom_call" | custom-call | tf_op jit(solution)/shard_map/second/pallas_call | solution.py:677
Async XLA Ops:
  2.3 15.2 %collective-permute-start.1 = (f32[776,128]{1,0:T(8,128)S(1)}, f32[776,128]{1,0:T(8,128)S(1)}, u32[]{:S(2)}, u32[]{:S(2)}) collective-permute-start(f32[776,128]{1,0:T(8,128)S(1)} %get-tuple-element.38), channel_id=1, source_target_pairs={{1,2},{3,4},{5,6},{7,8},{9,10},{11,12},{13,14},{2,1},{4,3},{6,5},{... | collective-permute-start | bytes 1191944 | tf_op jit(solution)/shard_map/ppermute | solution.py:652
  4.5 13.0 %collective-permute-start = (f32[12,64,128]{2,1,0:T(8,128)S(1)}, f32[12,64,128]{2,1,0:T(8,128)S(1)}, u32[]{:S(2)}, u32[]{:S(2)}) collective-permute-start(f32[12,64,128]{2,1,0:T(8,128)S(1)} %get-tuple-element.37), channel_id=1, source_target_pairs={{0,1},{1,0},{2,3},{3,2},{4,5},{5,4},{6,7},{7,6},{8,9},{9,8},{10,11... | collective-permute-start | bytes 1179656 | tf_op jit(solution)/shard_map/ppermute | solution.py:653
  8.9 9.3 %all-to-all-start = ((f32[16,8,128]{2,1,0:T(8,128)}), f32[16,8,128]{2,1,0:T(8,128)S(1)}, u32[]{:S(2)}, u32[]{:S(2)}) async-start(f32[16,8,128]{2,1,0:T(8,128)} %get-tuple-element.36), calls=%async_computation | async-start | bytes 131072 | tf_op jit(solution)/shard_map/all_to_all | solution.py:654
